TPU v7x, 32 devices: a whole 2x2x4 slice. The times are simulated.
32 devices in a mesh: dp: 16 (over z, y, x), mp: 2 (over core).
Axes of the slice: x: 2, y: 2, z: 4, core: 2. Of those that a mesh axis runs over, the one named last changes fastest.
Arguments:
- tokens: bfloat16 [16384, 768], P('dp'), may hold values from -6 to 6
- cotangent: bfloat16 [16384, 768], P('dp'), may hold values from -6 to 6
- lengths: int32 [16, 24], P('dp'), may hold values from 1 to 200, 1024 in all within a row
- query_weight: bfloat16 [768, 768], P(None, 'mp'), may hold values from -0.21875 to 0.21875
- query_bias: float32 [768], P('mp'), may hold values from -3 to 3
- key_weight: bfloat16 [768, 768], P(None, 'mp'), may hold values from -0.21875 to 0.21875
- value_weight: bfloat16 [768, 768], P(None, 'mp'), may hold values from -0.21875 to 0.21875
- value_bias: float32 [768], P('mp'), may hold values from -3 to 3
- output_weight: bfloat16 [768, 768], P('mp'), may hold values from -1.25 to 1.25
- output_bias: float32 [768], replicated, may hold values from -3 to 3
- first_gain: float32 [768], replicated, may hold values from 0.5 to 1.5
- first_shift: float32 [768], replicated, may hold values from -3 to 3
- up_weight: bfloat16 [768, 3072], P(None, 'mp'), may hold values from -0.21875 to 0.21875
- up_bias: float32 [3072], P('mp'), may hold values from -3 to 3
- down_weight: bfloat16 [3072, 768], P('mp'), may hold values from -0.21875 to 0.21875
- down_bias: float32 [768], replicated, may hold values from -3 to 3
- second_gain: float32 [768], replicated, may hold values from 0.5 to 1.5
- second_shift: float32 [768], replicated, may hold values from -3 to 3
Outputs:
- layer_output: bfloat16 [16384, 768], P('dp')
- tokens_grad: bfloat16 [16384, 768], P('dp')
- query_weight_grad: float32 [768, 768], P(None, 'mp')
- query_bias_grad: float32 [768], P('mp')
- key_weight_grad: float32 [768, 768], P(None, 'mp')
- value_weight_grad: float32 [768, 768], P(None, 'mp')
- value_bias_grad: float32 [768], P('mp')
- output_weight_grad: float32 [768, 768], P('mp')
- output_bias_grad: float32 [768], replicated
- first_gain_grad: float32 [768], replicated
- first_shift_grad: float32 [768], replicated
- up_weight_grad: float32 [768, 3072], P(None, 'mp')
- up_bias_grad: float32 [3072], P('mp')
- down_weight_grad: float32 [3072, 768], P('mp')
- down_bias_grad: float32 [768], replicated
- second_gain_grad: float32 [768], replicated
- second_shift_grad: float32 [768], replicated
Inputs may be any that keep to these rules, and one draw needn't show every extreme that they name: Each row holds the lengths of the 23 sequences packed on one index of dp, in order, then the length of its padding run; each row sums to 1024 and its largest entry is 200.
All inputs are finite; a program needn't handle non-finite values.
Results may differ from a plain program's by a relative error of at most 0.024.
Values may be sent and summed in bfloat16 or wider, within the bound.
A program may use at most 192 MiB of HBM per device.

v0:
```python
import math

import jax
import jax.numpy as jnp
from jax import lax
from jax.sharding import PartitionSpec as P

HEAD_DIM = 64


EPSILON = 1e-12
NEGATIVE = -1e30


def layer_norm(hidden, norm_gain, norm_shift):
    row_mean = jnp.mean(hidden, axis=-1, keepdims=True)
    centered = hidden - row_mean
    variance = jnp.mean(centered * centered, axis=-1, keepdims=True)
    return centered * lax.rsqrt(variance + EPSILON) * norm_gain + norm_shift


def gelu_exact(pre_act):
    return jax.nn.gelu(pre_act, approximate=False)


def contract_rows(left, right):
    return lax.dot_general(
        left, right, (((0,), (0,)), ((), ())), preferred_element_type=jnp.float32
    )


def times_transposed(left, right):
    return lax.dot_general(
        left, right, (((1,), (1,)), ((), ())), preferred_element_type=jnp.float32
    )


def masked_scores(query_heads, key_heads, same_segment, score_scale):
    raw_scores = (
        jnp.einsum("qhd,khd->hqk", query_heads, key_heads, preferred_element_type=jnp.float32)
        * score_scale
    )
    return jnp.where(same_segment[None], raw_scores, NEGATIVE)


def local(
    tokens,
    cotangent,
    lengths,
    query_weight,
    query_bias,
    key_weight,
    value_weight,
    value_bias,
    output_weight,
    output_bias,
    first_gain,
    first_shift,
    up_weight,
    up_bias,
    down_weight,
    down_bias,
    second_gain,
    second_shift,
):
    row_count = tokens.shape[0]
    shard_width = query_weight.shape[1]
    heads_shard = shard_width // HEAD_DIM
    score_scale = 1.0 / math.sqrt(HEAD_DIM)
    seq_ends = jnp.cumsum(lengths[0])
    places = jnp.arange(row_count, dtype=jnp.int32)
    segment = jnp.sum((places[:, None] >= seq_ends[None, :]).astype(jnp.int32), axis=1)
    same_segment = segment[:, None] == segment[None, :]
    live_rows = (segment < lengths.shape[1] - 1).astype(jnp.float32)
    tokens_wide = tokens.astype(jnp.float32)
    query = (jnp.dot(tokens, query_weight, preferred_element_type=jnp.float32) + query_bias).astype(
        jnp.bfloat16
    )
    key_part = jnp.dot(tokens, key_weight, preferred_element_type=jnp.float32).astype(jnp.bfloat16)
    value_part = (
        jnp.dot(tokens, value_weight, preferred_element_type=jnp.float32) + value_bias
    ).astype(jnp.bfloat16)
    query_heads = query.reshape(row_count, heads_shard, HEAD_DIM)
    key_heads = key_part.reshape(row_count, heads_shard, HEAD_DIM)
    value_heads = value_part.reshape(row_count, heads_shard, HEAD_DIM)
    scores = masked_scores(query_heads, key_heads, same_segment, score_scale)
    log_total = jax.nn.logsumexp(scores, axis=-1, keepdims=True)
    probabilities = jnp.exp(scores - log_total)
    context = jnp.einsum(
        "hqk,khd->qhd",
        probabilities.astype(jnp.bfloat16),
        value_heads,
        preferred_element_type=jnp.float32,
    )
    context = context.reshape(row_count, shard_width).astype(jnp.bfloat16)
    attention = lax.psum(
        jnp.dot(context, output_weight, preferred_element_type=jnp.float32).astype(jnp.bfloat16),
        "mp",
    ).astype(jnp.float32)
    hidden = tokens_wide + attention + output_bias
    first, first_pull = jax.vjp(layer_norm, hidden, first_gain, first_shift)
    first_low = first.astype(jnp.bfloat16)
    inner, gelu_pull = jax.vjp(
        gelu_exact, jnp.dot(first_low, up_weight, preferred_element_type=jnp.float32) + up_bias
    )
    inner_low = inner.astype(jnp.bfloat16)
    feed = lax.psum(
        jnp.dot(inner_low, down_weight, preferred_element_type=jnp.float32).astype(jnp.bfloat16),
        "mp",
    ).astype(jnp.float32)
    result, second_pull = jax.vjp(layer_norm, first + feed + down_bias, second_gain, second_shift)
    grad_out = cotangent.astype(jnp.float32) * live_rows[:, None]
    d_resid, second_gain_grad, second_shift_grad = second_pull(grad_out)
    down_bias_grad = jnp.sum(d_resid, axis=0)
    feed_grad = d_resid.astype(jnp.bfloat16)
    down_weight_grad = contract_rows(inner_low, feed_grad)
    d_inner = times_transposed(feed_grad, down_weight)
    d_pre = gelu_pull(d_inner)[0].astype(jnp.bfloat16)
    up_weight_grad = contract_rows(first_low, d_pre)
    up_bias_grad = jnp.sum(d_pre.astype(jnp.float32), axis=0)
    d_first = d_resid + lax.psum(
        times_transposed(d_pre, up_weight).astype(jnp.bfloat16), "mp"
    ).astype(jnp.float32)
    d_hidden, first_gain_grad, first_shift_grad = first_pull(d_first)
    output_bias_grad = jnp.sum(d_hidden, axis=0)
    hidden_grad = d_hidden.astype(jnp.bfloat16)
    output_weight_grad = contract_rows(context, hidden_grad)
    d_context = times_transposed(hidden_grad, output_weight).astype(jnp.bfloat16)
    d_context = d_context.reshape(row_count, heads_shard, HEAD_DIM)
    probabilities = jnp.exp(
        masked_scores(query_heads, key_heads, same_segment, score_scale) - log_total
    )
    d_values = jnp.einsum(
        "hqk,qhd->khd",
        probabilities.astype(jnp.bfloat16),
        d_context,
        preferred_element_type=jnp.float32,
    ).astype(jnp.bfloat16)
    d_probs = jnp.einsum("qhd,khd->hqk", d_context, value_heads, preferred_element_type=jnp.float32)
    d_scores = probabilities * (d_probs - jnp.sum(d_probs * probabilities, axis=-1, keepdims=True))
    d_scores = d_scores.astype(jnp.bfloat16)
    d_query = (
        (
            jnp.einsum("hqk,khd->qhd", d_scores, key_heads, preferred_element_type=jnp.float32)
            * score_scale
        )
        .astype(jnp.bfloat16)
        .reshape(row_count, shard_width)
    )
    d_keys = (
        (
            jnp.einsum("hqk,qhd->khd", d_scores, query_heads, preferred_element_type=jnp.float32)
            * score_scale
        )
        .astype(jnp.bfloat16)
        .reshape(row_count, shard_width)
    )
    d_values = d_values.reshape(row_count, shard_width)
    query_weight_grad = contract_rows(tokens, d_query)
    key_weight_grad = contract_rows(tokens, d_keys)
    value_weight_grad = contract_rows(tokens, d_values)
    query_bias_grad = jnp.sum(d_query.astype(jnp.float32), axis=0)
    value_bias_grad = jnp.sum(d_values.astype(jnp.float32), axis=0)
    token_part = (
        times_transposed(d_query, query_weight)
        + times_transposed(d_keys, key_weight)
        + times_transposed(d_values, value_weight)
    )
    tokens_grad = (
        d_hidden + lax.psum(token_part.astype(jnp.bfloat16), "mp").astype(jnp.float32)
    ).astype(jnp.bfloat16)
    (
        query_weight_grad,
        query_bias_grad,
        key_weight_grad,
        value_weight_grad,
        value_bias_grad,
        output_weight_grad,
        output_bias_grad,
        first_gain_grad,
        first_shift_grad,
        up_weight_grad,
        up_bias_grad,
        down_weight_grad,
        down_bias_grad,
        second_gain_grad,
        second_shift_grad,
    ) = lax.psum(
        (
            query_weight_grad,
            query_bias_grad,
            key_weight_grad,
            value_weight_grad,
            value_bias_grad,
            output_weight_grad,
            output_bias_grad,
            first_gain_grad,
            first_shift_grad,
            up_weight_grad,
            up_bias_grad,
            down_weight_grad,
            down_bias_grad,
            second_gain_grad,
            second_shift_grad,
        ),
        "dp",
    )
    return (
        result.astype(jnp.bfloat16),
        tokens_grad,
        query_weight_grad,
        query_bias_grad,
        key_weight_grad,
        value_weight_grad,
        value_bias_grad,
        output_weight_grad,
        output_bias_grad,
        first_gain_grad,
        first_shift_grad,
        up_weight_grad,
        up_bias_grad,
        down_weight_grad,
        down_bias_grad,
        second_gain_grad,
        second_shift_grad,
    )


def solution(mesh):
    in_specs = (
        P("dp", None),
        P("dp", None),
        P("dp", None),
        P(None, "mp"),
        P("mp"),
        P(None, "mp"),
        P(None, "mp"),
        P("mp"),
        P("mp", None),
        P(),
        P(),
        P(),
        P(None, "mp"),
        P("mp"),
        P("mp", None),
        P(),
        P(),
        P(),
    )
    out_specs = (
        P("dp", None),
        P("dp", None),
        P(None, "mp"),
        P("mp"),
        P(None, "mp"),
        P(None, "mp"),
        P("mp"),
        P("mp", None),
        P(),
        P(),
        P(),
        P(None, "mp"),
        P("mp"),
        P("mp", None),
        P(),
        P(),
        P(),
    )
    return jax.shard_map(local, mesh=mesh, in_specs=in_specs, out_specs=out_specs, check_vma=False)
```

profile of v0, /device:TPU:0, one launch (start us, length us, event | category | flops | bytes accessed | tf_op | source)
XLA Modules:
  0.0 700.9 jit_solution(12587975297367712340)
XLA Ops:
  7.3 0.9 copy.51
  8.2 0.1 reduce.2
  8.3 0.1 convert_reduce_fusion.3
  8.4 0.7 broadcast_compare_fusion
  9.1 2.3 convolution_convert_fusion.4
  11.5 0.8 add_convert_fusion.6
  12.3 10.6 %fusion = (f32[6,1024]{1,0:T(8,128)S(1)}, f32[6,1024,1024]{1,2,0:T(8,128)}) fusion(pred[1024,1024]{0,1:T(8,128)(4,1)S(1)} %broadcast_compare_fusion, bf16[1024,6,64]{0,2,1:T(8,128)(2,1)S(1)} %bitcast.65, bf16[1024,6,64]{0,2,1:T(8,128)(2,1)S(1)} %bitcast.67), kind=kOutput, calls=%fused_computation.5 | convolution fusion | flops 824174592 | bytes 27811840 | tf_op jit(solution)/shard_map/qhd,khd->hqk/dot_general | solution.py:40
  22.9 11.3 %exponential_reduce_fusion = f32[6,1024]{1,0:T(8,128)S(1)} fusion(f32[6,1024,1024]{1,2,0:T(8,128)} %get-tuple-element.102, f32[6,1024]{1,0:T(8,128)S(1)} %is-finite_select_fusion, pred[1024,1024]{0,1:T(8,128)(4,1)S(1)} %broadcast_compare_fusion), kind=kLoop, calls=%fused_computation.3 | loop fusion | flops 25159680 | bytes 26263552 | tf_op jit(solution)/shard_map/reduce_sum | solution.py:87
  34.3 0.8 add_convert_fusion.7
  35.2 11.8 %convolution_convert_fusion.6 = bf16[6,64,1024]{2,1,0:T(8,128)(2,1)S(1)} fusion(bf16[1024,6,64]{0,2,1:T(8,128)(2,1)S(1)} %bitcast.77, f32[6,1024,1024]{1,2,0:T(8,128)} %get-tuple-element.102, f32[6,1024]{1,0:T(8,128)S(1)} %log_add_fusion, pred[1024,1024]{0,1:T(8,128)(4,1)S(1)} %broadcast_compare_fusion), kind=kOutput, calls=%fused_computation.66 | convolution fusion | flops 830865408 | bytes 27811840 | tf_op jit(solution)/shard_map/hqk,khd->qhd/dot_general | solution.py:89
  47.0 0.9 copy-done.43
  47.9 2.2 convolution_convert_fusion
  50.1 0.5 all-reduce.10.cloned.1.call-start
  50.6 22.7 %all-reduce.8.cloned.1.call-done = bf16[1024,768]{1,0:T(8,128)(2,1)} async-done(((bf16[1024,768]{1,0:T(8,128)(2,1)}), bf16[1024,768]{1,0:T(8,128)(2,1)}) %all-reduce.8.cloned.1.call-update) | async-done | bytes 1572880 | tf_op jit(solution)/shard_map/psum | solution.py:96
  73.4 2.6 fusion.11
  76.0 0.2 copy-done.5
  76.2 0.9 multiply_reduce_fusion.6
  77.1 17.9 %multiply_convert_fusion.1 = (bf16[1024,1536]{1,0:T(8,128)(2,1)S(1)}, f32[1024,1536]{1,0:T(8,128)}, f32[1024,1536]{1,0:T(8,128)}) fusion(f32[1536]{0:T(1024)S(1)} %copy-done.40, bf16[768,1536]{1,0:T(8,128)(2,1)S(1)} %copy-done, f32[768]{0:T(1024)S(1)} %copy-done.35, f32[768]{0:T(1024)S(1)} %copy-done.31, f32[1024]{0:T(1024)S(1)} %fusion.13, ...), kind=kOutput, calls=%fused_computation.11 | convolution fusion | flops 2526806016 | bytes 21257216 | tf_op jit(solution)/shard_map/dot_general | solution.py:104
  95.0 1.7 copy-done.46
  96.6 3.7 convolution_convert_fusion.2
  100.4 21.7 %all-reduce.10.cloned.1.call-done = bf16[1024,768]{1,0:T(8,128)(2,1)} async-done(((bf16[1024,768]{1,0:T(8,128)(2,1)}), bf16[1024,768]{1,0:T(8,128)(2,1)}) %all-reduce.10.cloned.1.call-update) | async-done | bytes 1572880 | tf_op jit(solution)/shard_map/psum | solution.py:107
  122.1 3.6 fusion.29
  125.7 0.5 multiply_reduce_fusion.5
  126.2 0.8 copy-done.11
  127.0 1.7 multiply_reduce_fusion.1
  128.8 2.8 fusion.28
  131.6 8.0 %convert_reduce_fusion = (f32[1536]{0:T(1024)S(1)}, bf16[1024,1536]{1,0:T(8,128)(2,1)S(1)}) fusion(f32[1024,1536]{1,0:T(8,128)S(1)} %bitcast.85, bf16[1536,768]{1,0:T(8,128)(2,1)S(1)} %copy-done.37, f32[1024,768]{1,0:T(8,128)S(1)} %get-tuple-element.93, f32[1024]{0:T(1024)S(1)} %negate_multiply_fusion.2, f32[1024,1536]{1,0:T(8,128)} %get-tuple-element.103, ...), kind=kOutput, calls=%fused_computation.9 | convolution fusion | flops 2444229120 | bytes 21250048 | tf_op jit(solution)/shard_map/dot_general | solution.py:33
  139.6 1.7 copy-done.45
  141.3 3.7 convolution_convert_fusion.1
  145.1 8.1 %fusion.20 = f32[768,1536]{1,0:T(8,128)} fusion(bf16[1024,1536]{1,0:T(8,128)(2,1)} %copy-done.45, f32[768]{0:T(1024)S(1)} %copy-done.35, f32[768]{0:T(1024)S(1)} %copy-done.31, f32[1024]{0:T(1024)S(1)} %fusion.13, bf16[1024,768]{1,0:T(8,128)(2,1)} %all-reduce.8.cloned.1.call-done, bf16[1024,768]{1,0:T(8,128)(2,1)} %param.18, ...), kind=kOutput, calls=%fused_computation.85 | convolution fusion | flops 2422996992 | bytes 11027456 | tf_op jit(solution)/shard_map/dot_general | solution.py:27
  153.2 13.6 %all-reduce.12.cloned.1.call-done = bf16[1024,768]{1,0:T(8,128)(2,1)} async-done(((bf16[1024,768]{1,0:T(8,128)(2,1)}), bf16[1024,768]{1,0:T(8,128)(2,1)}) %all-reduce.12.cloned.1.call-update) | async-done | bytes 1572880 | tf_op jit(solution)/shard_map/psum | solution.py:121
  166.8 4.8 multiply_reduce_fusion.2
  171.7 2.1 fusion.27
  173.8 1.6 copy-done.9
  175.4 0.9 convolution_convert_fusion.3
  176.3 0.9 copy-done.24
  177.2 12.6 %convert_reduce_fusion.1 = (f32[6,64]{1,0:T(8,128)S(1)}, bf16[6,64,1024]{2,1,0:T(8,128)(2,1)}) fusion(bf16[1024,6,64]{0,2,1:T(8,128)(2,1)S(1)} %bitcast.79, f32[6,1024,1024]{1,2,0:T(8,128)} %get-tuple-element.102, f32[6,1024]{1,0:T(8,128)S(1)} %log_add_fusion, pred[1024,1024]{0,1:T(8,128)(4,1)S(1)} %broadcast_compare_fusion), kind=kOutput, calls=%fused_computation.54 | convolution fusion | flops 831651456 | bytes 27813376 | tf_op jit(solution)/shard_map/hqk,qhd->khd/dot_general | solution.py:133
  189.8 17.1 %multiply_reduce_fusion = (f32[6,1024]{1,0:T(8,128)S(1)}, f32[6,1024,1024]{1,2,0:T(8,128)}) fusion(f32[6,1024,1024]{1,2,0:T(8,128)} %get-tuple-element.102, f32[6,1024]{1,0:T(8,128)S(1)} %log_add_fusion, pred[1024,1024]{0,1:T(8,128)(4,1)S(1)} %broadcast_compare_fusion, bf16[1024,6,64]{0,2,1:T(8,128)(2,1)} %bitcast.80, bf16[1024,6,64]{0,2,1:T(8,128)(2,1)S(1)} %bitcast.78), kind=kOutput, calls=%fused_computation.1 | convolution fusion | flops 836757504 | bytes 53002240 | tf_op jit(solution)/shard_map/qhd,khd->hqk/dot_general | solution.py:139
  206.9 21.7 %multiply_convert_fusion = bf16[6,1024,1024]{1,2,0:T(8,128)(2,1)} fusion(f32[6,1024,1024]{1,2,0:T(8,128)} %get-tuple-element.105, f32[6,1024,1024]{1,2,0:T(8,128)} %get-tuple-element.102, f32[6,1024]{1,0:T(8,128)S(1)} %get-tuple-element.104, f32[6,1024]{1,0:T(8,128)S(1)} %log_add_fusion, pred[1024,1024]{0,1:T(8,128)(4,1)S(1)} %broadcast_compare_fusion), kind=kLoop, calls=%fused_computation | loop fusion | flops 37748736 | bytes 64012288 | tf_op jit(solution)/shard_map/convert_element_type | solution.py:141
  228.6 8.6 %multiply_convert_fusion.2 = bf16[6,64,1024]{2,1,0:T(8,128)(2,1)S(1)} fusion(bf16[1024,6,64]{0,2,1:T(8,128)(2,1)S(1)} %bitcast.66, bf16[6,1024,1024]{1,2,0:T(8,128)(2,1)} %multiply_convert_fusion), kind=kOutput, calls=%fused_computation.56 | convolution fusion | flops 806092800 | bytes 14155776 | tf_op jit(solution)/shard_map/hqk,qhd->khd/dot_general | solution.py:152
  237.2 7.0 convert_reduce_fusion.2
  244.2 1.0 fusion.32
  245.2 1.0 fusion.31
  246.3 0.1 copy-done.20
  246.4 0.2 copy-done.29
  246.5 2.2 add_convert_fusion.2
  248.7 0.3 all-reduce.16.cloned.1.call-start
  249.0 7.9 %fusion.15 = f32[1536,768]{1,0:T(8,128)} fusion(bf16[1024,1536]{1,0:T(8,128)(2,1)} %copy-done.46, f32[1024,768]{1,0:T(8,128)} %copy-done.7, f32[1024]{0:T(1024)S(1)} %negate_multiply_fusion.2), kind=kOutput, calls=%fused_computation.82 | convolution fusion | flops 2417491968 | bytes 11014144 | tf_op jit(solution)/shard_map/dot_general | solution.py:27
  256.9 1.8 convolution_bitcast_fusion
  258.7 1.8 convolution_bitcast_fusion.2
  260.5 1.8 convolution_bitcast_fusion.1
  262.3 0.5 copy-done.10
  262.7 0.2 copy-done.44
  263.0 2.0 fusion.17
  265.1 5.4 all-reduce.14.cloned.1.call-done
  270.5 4.0 add_reduce_fusion
  274.5 82.0 %all-reduce = (f32[384]{0:T(512)}, f32[384]{0:T(512)}, f32[768]{0:T(1024)}, f32[768]{0:T(1024)}, f32[768]{0:T(1024)}, /*index=5*/f32[1536]{0:T(1024)}, f32[768]{0:T(1024)}, f32[768]{0:T(1024)}, f32[768]{0:T(1024)}) all-reduce(f32[384]{0:T(512)S(1)} %reduce_sum.228, f32[384]{0:T(512)S(1)} %reduce_sum.230, ...), channel_id=1, replica_groups=mesh['dp'=16,'mp'=2] {'dp'}, use_global_device_ids=true, to_apply=%region_19.20 | all-reduce | flops 6912 | bytes 55296 | tf_op jit(solution)/shard_map/psum | solution.py:188
  356.5 323.2 %all-reduce.16.cloned.1.call-done = (f32[768,384]{0,1:T(8,128)}, f32[768,384]{0,1:T(8,128)}, f32[768,384]{0,1:T(8,128)}, f32[384,768]{1,0:T(8,128)}, f32[768,1536]{1,0:T(8,128)}, /*index=5*/f32[1536,768]{1,0:T(8,128)}) async-done(((f32[768,384]{0,1:T(8,128)}, f32[768,384]{0,1:T(8,128)}, f32[768,384]{0,1:T(8,128)}, f32[384,768]{1,0:T(8,128)}, f32[768,1536]{1,0:T(8,128)}, /*index=5*/f32[1536,768]{1,0:T(8,128)}), ...) | async-done | bytes 14155792 | tf_op jit(solution)/shard_map/psum | solution.py:188
  679.6 2.8 copy.56
  682.4 1.4 copy.57
  683.8 1.4 copy.58
  685.2 1.0 copy.73
  686.2 5.5 copy.74
  691.8 2.2 copy.75
  (115 shorter events, 0.7 us)
Async XLA Ops:
  7.2 69.9 %copy-start = (bf16[768,1536]{1,0:T(8,128)(2,1)S(1)}, bf16[768,1536]{1,0:T(8,128)(2,1)}, u32[]{:S(2)}) copy-start(bf16[768,1536]{1,0:T(8,128)(2,1)} %param.30) | copy-start | bytes 7077892
  7.2 4.2 copy-start.41
  7.2 66.1 %all-reduce.8.cloned.1.call-start = ((), (), s32[]{:S(2)}) async-start(), calls=%async_computation | async-start | bytes 3145728 | tf_op jit(solution)/shard_map/psum | solution.py:96
  8.3 3.1 copy-start.2
  8.3 3.1 copy-start.26
  11.5 11.4 %copy-start.15 = (bf16[1024,384]{0,1:T(8,128)(2,1)}, bf16[1024,384]{0,1:T(8,128)(2,1)S(1)}, u32[]{:S(2)}) copy-start(bf16[1024,384]{0,1:T(8,128)(2,1)S(1)} %convolution_convert_fusion.4) | copy-start | bytes 2359300
  12.3 10.6 %copy-start.13 = (bf16[1024,384]{0,1:T(8,128)(2,1)}, bf16[1024,384]{0,1:T(8,128)(2,1)S(1)}, u32[]{:S(2)}) copy-start(bf16[1024,384]{0,1:T(8,128)(2,1)S(1)} %add_convert_fusion.6) | copy-start | bytes 2359300
  22.9 11.4 %copy-start.28 = (bf16[768,384]{1,0:T(8,128)(2,1)S(1)}, bf16[768,384]{1,0:T(8,128)(2,1)}, u32[]{:S(2)}) copy-start(bf16[768,384]{1,0:T(8,128)(2,1)} %param.24) | copy-start | bytes 1769476
  22.9 11.4 %copy-start.42 = (f32[384]{0:T(512)S(1)}, f32[384]{0:T(512)}, u32[]{:S(2)}) copy-start(f32[384]{0:T(512)} %param.25) | copy-start | bytes 4612
  35.2 11.8 %copy-start.22 = (bf16[1024,384]{0,1:T(8,128)(2,1)}, bf16[1024,384]{0,1:T(8,128)(2,1)S(1)}, u32[]{:S(2)}) copy-start(bf16[1024,384]{0,1:T(8,128)(2,1)S(1)} %add_convert_fusion.7) | copy-start | bytes 2359300
  35.2 12.7 %copy-start.38 = (bf16[384,768]{1,0:T(8,128)(2,1)S(1)}, bf16[384,768]{1,0:T(8,128)(2,1)}, u32[]{:S(2)}) copy-start(bf16[384,768]{1,0:T(8,128)(2,1)} %param.26) | copy-start | bytes 1769476
  47.0 0.9 copy-start.43
  47.0 26.4 %copy-start.30 = (f32[768]{0:T(1024)S(1)}, f32[768]{0:T(1024)}, u32[]{:S(2)}) copy-start(f32[768]{0:T(1024)} %param.27) | copy-start | bytes 9220
  50.1 27.0 %copy-start.31 = (f32[768]{0:T(1024)S(1)}, f32[768]{0:T(1024)}, u32[]{:S(2)}) copy-start(f32[768]{0:T(1024)} %param.28) | copy-start | bytes 9220
  50.1 27.0 %copy-start.35 = (f32[768]{0:T(1024)S(1)}, f32[768]{0:T(1024)}, u32[]{:S(2)}) copy-start(f32[768]{0:T(1024)} %param.29) | copy-start | bytes 9220
  50.1 27.0 %copy-start.40 = (f32[1536]{0:T(1024)S(1)}, f32[1536]{0:T(1024)}, u32[]{:S(2)}) copy-start(f32[1536]{0:T(1024)} %param.31) | copy-start | bytes 18436
  50.1 71.9 %all-reduce.10.cloned.1.call-start = ((), (), s32[]{:S(2)}) async-start(), calls=%async_computation.1 | async-start | bytes 3145728 | tf_op jit(solution)/shard_map/psum | solution.py:107
  73.4 2.6 copy-start.3
  73.4 2.8 copy-start.5
  77.1 19.5 %copy-start.36 = (bf16[1536,768]{1,0:T(8,128)(2,1)S(1)}, bf16[1536,768]{1,0:T(8,128)(2,1)}, u32[]{:S(2)}) copy-start(bf16[1536,768]{1,0:T(8,128)(2,1)} %param.32) | copy-start | bytes 7077892
  95.0 1.7 copy-start.46
  96.6 25.4 %copy-start.34 = (f32[768]{0:T(1024)S(1)}, f32[768]{0:T(1024)}, u32[]{:S(2)}) copy-start(f32[768]{0:T(1024)} %param.33) | copy-start | bytes 9220
  100.3 66.4 %all-reduce.12.cloned.1.call-start = ((), (), s32[]{:S(2)}) async-start(), calls=%async_computation.2 | async-start | bytes 3145728 | tf_op jit(solution)/shard_map/psum | solution.py:121
  122.1 9.5 %slice-start.2 = ((s8[6291456]{0:T(1024)(128)(4,1)}), s8[4194304]{0:T(1024)(128)(4,1)S(1)}, s32[]{:S(2)}) async-start(s8[6291456]{0:T(1024)(128)(4,1)} %bitcast.84), calls=%async_computation.7 | async-start | bytes 8388608
  125.6 1.4 copy-start.11
  125.6 1.4 copy-start.32
  126.2 2.6 copy-start.33
  127.0 4.5 slice-start.3
  128.7 2.8 copy-start.37
  131.5 8.1 %copy-start.7 = (f32[1024,768]{1,0:T(8,128)}, f32[1024,768]{1,0:T(8,128)S(1)}, u32[]{:S(2)}) copy-start(f32[1024,768]{1,0:T(8,128)S(1)} %get-tuple-element.93) | copy-start | bytes 9437188
  139.6 1.7 copy-start.45
  145.0 21.7 %copy-start.4 = (bf16[1024,768]{1,0:T(8,128)(2,1)S(1)}, bf16[1024,768]{1,0:T(8,128)(2,1)}, u32[]{:S(2)}) copy-start(bf16[1024,768]{1,0:T(8,128)(2,1)} %param.18) | copy-start | bytes 4718596
  145.0 125.4 %all-reduce.14.cloned.1.call-start = ((), (), s32[]{:S(2)}) async-start(), calls=%async_computation.3 | async-start | bytes 3145728 | tf_op jit(solution)/shard_map/psum | solution.py:170
  166.8 4.9 copy-start.6
  166.8 4.9 copy-start.8
  166.8 4.9 copy-start.12
  171.7 3.7 copy-start.39
  173.7 1.6 copy-start.9
  176.3 0.9 copy-start.24
  177.2 12.6 %copy-start.23 = (bf16[1024,384]{0,1:T(8,128)(2,1)S(1)}, bf16[1024,384]{0,1:T(8,128)(2,1)}, u32[]{:S(2)}) copy-start(bf16[1024,384]{0,1:T(8,128)(2,1)} %copy-done.22) | copy-start | bytes 2359300
  206.9 21.7 %copy-start.14 = (bf16[1024,384]{0,1:T(8,128)(2,1)S(1)}, bf16[1024,384]{0,1:T(8,128)(2,1)}, u32[]{:S(2)}) copy-start(bf16[1024,384]{0,1:T(8,128)(2,1)} %copy-done.13) | copy-start | bytes 2359300
  228.6 8.6 %copy-start.16 = (bf16[1024,384]{0,1:T(8,128)(2,1)S(1)}, bf16[1024,384]{0,1:T(8,128)(2,1)}, u32[]{:S(2)}) copy-start(bf16[1024,384]{0,1:T(8,128)(2,1)} %copy-done.15) | copy-start | bytes 2359300
  237.2 7.0 %copy-start.25 = (bf16[768,384]{1,0:T(8,128)(2,1)S(1)}, bf16[768,384]{1,0:T(8,128)(2,1)}, u32[]{:S(2)}) copy-start(bf16[768,384]{1,0:T(8,128)(2,1)} %param.23) | copy-start | bytes 1769476
  244.2 1.1 copy-start.27
  245.2 1.1 copy-start.20
  245.2 1.3 copy-start.29
  248.7 430.9 %all-reduce.16.cloned.1.call-start = ((), (), s32[]{:S(2)}) async-start(), calls=%async_computation.4 | async-start | bytes 28311552 | tf_op jit(solution)/shard_map/psum | solution.py:188
  249.0 7.9 %copy-start.21 = (bf16[6,64,1024]{2,1,0:T(8,128)(2,1)S(1)}, bf16[6,64,1024]{2,1,0:T(8,128)(2,1)}, u32[]{:S(2)}) copy-start(bf16[6,64,1024]{2,1,0:T(8,128)(2,1)} %get-tuple-element.109) | copy-start | bytes 2359300
  260.5 2.3 copy-start.10
  260.5 2.5 copy-start.44
  679.6 2.8 copy-start.19
  679.6 4.2 copy-start.18
  679.6 5.6 copy-start.17
  685.2 6.5 slice-start
  686.2 5.5 slice-start.1
  686.2 7.7 %copy-start.1 = (bf16[768,1536]{1,0:T(8,128)(2,1)S(1)}, bf16[768,1536]{1,0:T(8,128)(2,1)}, u32[]{:S(2)}) copy-start(bf16[768,1536]{1,0:T(8,128)(2,1)} %param.30) | copy-start | bytes 7077892
Sparse Core Ops, SparseCore 0:
  50.2 23.1 all-reduce.7
  100.4 21.5 all-reduce.9
  145.1 21.5 all-reduce.11
  248.8 21.5 all-reduce.13
  277.9 401.7 all-reduce.15
where the time goes:
time: 709 us; the launch traced here: 701 us
  waiting for transfers between devices  387 us (55%)
  matrix products  135 us (19%)
  blocking collectives  82 us (12%)
  other arithmetic  56.9 us (8%)
  local copies, waits for them, and re-layouts  24.3 us (3%)
  between operations  14.9 us (2%)
    psum x1, waiting for transfers between devices, local(): lax.psum((query_weight_grad, query_bias_grad, key_weight_grad, value_weig...  323 us
    psum x1, blocking collectives, local(): lax.psum((query_weight_grad, query_bias_grad, key_weight_grad, value_weig...  82 us
    dot_general x6, matrix products, contract_rows(): lax.dot_general(left, right, (((0,), (0,)), ((), ())), preferred_element_...  23.3 us
    unnamed x108, local copies, waits for them, and re-layouts  23.2 us
    psum x1, waiting for transfers between devices, local(): lax.psum(jnp.dot(context, output_weight, preferred_element_type=jnp.float...  22.7 us
    convert_element_type x1, other arithmetic, local(): d_scores = d_scores.astype(jnp.bfloat16)  21.7 us
    psum x1, waiting for transfers between devices, local(): lax.psum(jnp.dot(inner_low, down_weight, preferred_element_type=jnp.float...  21.7 us
    dot_general x1, matrix products, local(): jnp.dot(first_low, up_weight, preferred_element_type=jnp.float32) + up_bias  17.9 us
  transfers between devices with their start and end apart: 5, of which 5 were waited for; matrix products, arithmetic and copies ran while one was open for 4% of the time, Pallas kernels for 0%

commit v1 on v0

--- a/solution.py
+++ b/solution.py
@@ -1,15 +1,175 @@
+import functools
 import math
 
 import jax
 import jax.numpy as jnp
 from jax import lax
+from jax.experimental import pallas as pl
+from jax.experimental.pallas import tpu as pltpu
 from jax.sharding import PartitionSpec as P
 
 HEAD_DIM = 64
+MESH = pl.DeviceIdType.MESH
 
 
 EPSILON = 1e-12
 NEGATIVE = -1e30
+ROW_TILE = 16
+
+
+def bits_of(count):
+    bits, stride = [], 1
+    while stride < count:
+        bits.append(stride)
+        stride *= 2
+    return bits
+
+
+def exchange_orders(count):
+    bits = bits_of(count)
+    if len(bits) < 3:
+        return [bits, bits[::-1]]
+    return [[bits[0], bits[2], bits[1]] + bits[3:], [bits[1], bits[2], bits[0]] + bits[3:]]
+
+
+def plan_steps(rows, order):
+    halvings, wholes, length = [], [], rows
+    for stride in order:
+        if (length // 2) % ROW_TILE == 0 and length % 2 == 0:
+            length //= 2
+            halvings.append((stride, length, "halve"))
+        else:
+            wholes.append((stride, length, "whole"))
+    gathers = [(stride, sent, "gather") for stride, sent, _ in reversed(halvings)]
+    return halvings + wholes + gathers
+
+
+def landing_rows(steps):
+    return sum(sent for _, sent, kind in steps if kind != "gather")
+
+
+class Reduction:
+    def __init__(self, block, total, landing, send_sem, recv_sem, steps, rows, dp, mp):
+        self.total, self.landing, self.send_sem, self.recv_sem = total, landing, send_sem, recv_sem
+        self.steps, self.dp, self.mp = steps, dp, mp
+        self.held, self.base = block, 0
+        self.low, self.offset = 0, 0
+        self.copies, self.next_step = [], 0
+
+    def side(self, stride):
+        return (self.dp // stride) % 2
+
+    def advance(self):
+        step = self.next_step
+        if step > 0:
+            self.finish(step - 1)
+        if step < len(self.steps):
+            self.start(step)
+        self.next_step += 1
+
+    def start(self, step):
+        stride, sent, kind = self.steps[step]
+        side = self.side(stride)
+        if kind == "gather":
+            rows = pl.ds(pl.multiple_of(self.low, ROW_TILE), sent)
+            source, target = self.total.at[rows], self.total.at[rows]
+        else:
+            start = self.base + (1 - side) * sent if kind == "halve" else self.base
+            source = self.held.at[pl.ds(pl.multiple_of(start, ROW_TILE), sent)]
+            target = self.landing.at[pl.ds(self.offset, sent)]
+        copy = pltpu.make_async_remote_copy(
+            source,
+            target,
+            self.send_sem.at[step],
+            self.recv_sem.at[step],
+            device_id=(self.dp + stride - 2 * stride * side, self.mp),
+            device_id_type=MESH,
+        )
+        copy.start()
+        self.copies.append(copy)
+
+    def finish(self, step):
+        stride, sent, kind = self.steps[step]
+        side = self.side(stride)
+        self.copies[step].wait()
+        if kind == "gather":
+            self.low = self.low - side * sent
+            return
+        kept = self.base + side * sent if kind == "halve" else self.base
+        if kind == "halve":
+            self.low = self.low + side * sent
+        last = step + 1 == len(self.steps) or (
+            self.steps[step + 1][2] == "gather"
+        )
+        held, offset, low = self.held, self.offset, self.low
+        part = sent
+        while part > 64 and part % 2 == 0 and (part // 2) % ROW_TILE == 0:
+            part //= 2
+
+        def add(index, carry):
+            own = pl.ds(pl.multiple_of(kept + index * part, ROW_TILE), part)
+            came = pl.ds(pl.multiple_of(offset + index * part, ROW_TILE), part)
+            both = held[own].astype(jnp.float32) + self.landing[came].astype(jnp.float32)
+            if last:
+                done = pl.ds(pl.multiple_of(low + index * part, ROW_TILE), part)
+                self.total[done] = both.astype(self.total.dtype)
+            else:
+                self.landing[came] = both.astype(self.landing.dtype)
+            return carry
+
+        lax.fori_loop(0, sent // part, add, 0)
+        self.held, self.base = self.landing, offset
+        self.offset += sent
+
+
+def reduce_kernel(plans, schedule, strides, *refs):
+    count = len(plans)
+    parts, sums, landings = refs[:count], refs[count : 2 * count], refs[2 * count : 3 * count]
+    send_sems, recv_sems = refs[3 * count : 4 * count], refs[4 * count : 5 * count]
+    dp, mp = lax.axis_index("dp"), lax.axis_index("mp")
+    barrier = pltpu.get_barrier_semaphore()
+    for stride in strides:
+        partner = dp + stride - 2 * stride * ((dp // stride) % 2)
+        pl.semaphore_signal(barrier, inc=1, device_id=(partner, mp), device_id_type=MESH)
+    pl.semaphore_wait(barrier, len(strides))
+    chains = [
+        Reduction(parts[c], sums[c], landings[c], send_sems[c], recv_sems[c], plans[c], parts[c].shape[0], dp, mp)
+        for c in range(count)
+    ]
+    for c in schedule:
+        chains[c].advance()
+
+
+def sum_over_dp(blocks, vectors, dp_size):
+    if dp_size == 1:
+        return blocks, vectors
+    orders = exchange_orders(dp_size)
+    arrays = list(blocks) + [vectors]
+    plans = [plan_steps(b.shape[0], orders[i % 2]) for i, b in enumerate(blocks)]
+    plans.append([(stride, vectors.shape[0], "whole") for stride in orders[0]])
+    begin = [i // 2 for i in range(len(blocks))] + [0]
+    schedule = []
+    for turn in range(max(begin) + max(len(p) for p in plans) + 1):
+        for c, plan in enumerate(plans):
+            if 0 <= turn - begin[c] <= len(plan):
+                schedule.append(c)
+    vmem = pl.BlockSpec(memory_space=pltpu.VMEM)
+    landing = [
+        pltpu.VMEM((landing_rows(plan), a.shape[1]), a.dtype) for plan, a in zip(plans, arrays)
+    ]
+    sems = [pltpu.SemaphoreType.DMA((len(plan),)) for plan in plans]
+    sums = pl.pallas_call(
+        functools.partial(reduce_kernel, plans, schedule, bits_of(dp_size)),
+        out_shape=[jax.ShapeDtypeStruct(a.shape, a.dtype) for a in arrays],
+        in_specs=[vmem] * len(arrays),
+        out_specs=[vmem] * len(arrays),
+        scratch_shapes=landing + sems + sems,
+        compiler_params=pltpu.CompilerParams(
+            collective_id=0, has_side_effects=True, vmem_limit_bytes=48 * 2**20
+        ),
+        name="sum_over_dp",
+    )(*arrays)
+    return sums[:-1], sums[-1]
 
 
 def layer_norm(hidden, norm_gain, norm_shift):
@@ -169,41 +329,65 @@
     tokens_grad = (
         d_hidden + lax.psum(token_part.astype(jnp.bfloat16), "mp").astype(jnp.float32)
     ).astype(jnp.bfloat16)
-    (
-        query_weight_grad,
+    half = shard_width
+    low = lambda grad: grad.astype(jnp.bfloat16)
+    attention_side = [
+        jnp.concatenate([low(query_weight_grad), low(key_weight_grad)], axis=1),
+        jnp.concatenate(
+            [
+                low(value_weight_grad),
+                jnp.concatenate(
+                    [low(output_weight_grad[:, :half]), low(output_weight_grad[:, half:])], axis=0
+                ),
+            ],
+            axis=1,
+        ),
+    ]
+    width = tokens.shape[1]
+    up_low, down_low = low(up_weight_grad), low(down_weight_grad)
+    blocks = [
+        down_low[:width],
+        down_low[width:],
+        up_low[:, :width],
+        up_low[:, width:],
+        *attention_side,
+    ]
+    vectors = [
         query_bias_grad,
-        key_weight_grad,
-        value_weight_grad,
         value_bias_grad,
-        output_weight_grad,
         output_bias_grad,
         first_gain_grad,
         first_shift_grad,
-        up_weight_grad,
         up_bias_grad,
-        down_weight_grad,
         down_bias_grad,
         second_gain_grad,
         second_shift_grad,
-    ) = lax.psum(
-        (
-            query_weight_grad,
-            query_bias_grad,
-            key_weight_grad,
-            value_weight_grad,
-            value_bias_grad,
-            output_weight_grad,
-            output_bias_grad,
-            first_gain_grad,
-            first_shift_grad,
-            up_weight_grad,
-            up_bias_grad,
-            down_weight_grad,
-            down_bias_grad,
-            second_gain_grad,
-            second_shift_grad,
-        ),
-        "dp",
+    ]
+    sizes = [v.shape[0] for v in vectors]
+    flat = jnp.concatenate(vectors)
+    rows = -(-flat.shape[0] // (128 * ROW_TILE)) * ROW_TILE
+    flat = jnp.pad(flat, (0, rows * 128 - flat.shape[0])).reshape(rows, 128)
+    blocks, flat = sum_over_dp(blocks, flat, lax.axis_size("dp"))
+    flat = flat.reshape(-1)
+    starts = [sum(sizes[:i]) for i in range(len(sizes))]
+    (
+        query_bias_grad,
+        value_bias_grad,
+        output_bias_grad,
+        first_gain_grad,
+        first_shift_grad,
+        up_bias_grad,
+        down_bias_grad,
+        second_gain_grad,
+        second_shift_grad,
+    ) = [flat[a : a + n] for a, n in zip(starts, sizes)]
+    wide = lambda total: total.astype(jnp.float32)
+    down_weight_grad = jnp.concatenate([wide(blocks[0]), wide(blocks[1])], axis=0)
+    up_weight_grad = jnp.concatenate([wide(blocks[2]), wide(blocks[3])], axis=1)
+    query_weight_grad, key_weight_grad = wide(blocks[4][:, :half]), wide(blocks[4][:, half:])
+    value_weight_grad = wide(blocks[5][:, :half])
+    output_weight_grad = jnp.concatenate(
+        [wide(blocks[5][:half, half:]), wide(blocks[5][half:, half:])], axis=1
     )
     return (
         result.astype(jnp.bfloat16),

time: 709 us -> 445 us (0.63)
  waiting for transfers between devices: 387 us -> 60.6 us
  Pallas kernels: 0 us -> 138 us
  blocking collectives: 82 us -> 0 us
  other arithmetic: 56.9 us -> 68.4 us
  local copies, waits for them, and re-layouts: 24.3 us -> 17 us
    psum x1 -> x0, waiting for transfers between devices: 323 us -> none  [local(): lax.psum((query_weight_grad, query_bias_grad, key_weight_grad, value_weig...]
    pallas_call x0 -> x1, Pallas kernels: none -> 138 us  [sum_over_dp(): pl.pallas_call(functools.partial(reduce_kernel, plans, schedule, bits_of(...]
    psum x1 -> x0, blocking collectives: 82 us -> none  [local(): lax.psum((query_weight_grad, query_bias_grad, key_weight_grad, value_weig...]
    psum x1, waiting for transfers between devices: 13.6 us -> 0.01 us  [local(): lax.psum(times_transposed(d_pre, up_weight).astype(jnp.bfloat16), 'mp')]
    unnamed x108 -> x106, local copies, waits for them, and re-layouts: 23.2 us -> 9.87 us
    psum x1, waiting for transfers between devices: 5.35 us -> 15.9 us  [local(): lax.psum(token_part.astype(jnp.bfloat16), 'mp').astype(jnp.float32)]
    concatenate x0 -> x5, other arithmetic: none -> 8.68 us  [the longest x1 2.82 us: local(): up_weight_grad = jnp.concatenate([wide(blocks[2]), wide(blocks[3])], axis=1)]
  transfers between devices with their start and end apart: 5 -> 4, of which waited for: 5 -> 3; matrix products, arithmetic and copies ran while one was open for 4% -> 6% of each run, Pallas kernels for 0% -> 0%
where the time goes in v1:
time: 445 us; the launch traced here: 437 us
  matrix products  138 us (31%)
  Pallas kernels  138 us (31%)
  other arithmetic  68.4 us (15%)
  waiting for transfers between devices  60.6 us (14%)
  local copies, waits for them, and re-layouts  17 us (4%)
  between operations  14.9 us (3%)
    pallas_call x1, Pallas kernels, sum_over_dp(): pl.pallas_call(functools.partial(reduce_kernel, plans, schedule, bits_of(...  138 us
    psum x1, waiting for transfers between devices, local(): lax.psum(jnp.dot(context, output_weight, preferred_element_type=jnp.float...  22.9 us
    dot_general x6, matrix products, contract_rows(): lax.dot_general(left, right, (((0,), (0,)), ((), ())), preferred_element_...  22.7 us
    convert_element_type x1, other arithmetic, local(): d_scores = d_scores.astype(jnp.bfloat16)  21.7 us
    psum x1, waiting for transfers between devices, local(): lax.psum(jnp.dot(inner_low, down_weight, preferred_element_type=jnp.float...  21.7 us
    dot_general x6, matrix products, times_transposed(): lax.dot_general(left, right, (((1,), (1,)), ((), ())), preferred_element_...  19.8 us
    dot_general x1, matrix products, local(): jnp.dot(first_low, up_weight, preferred_element_type=jnp.float32) + up_bias  17.9 us
    dot_general x1, matrix products, local(): jnp.einsum('qhd,khd->hqk', d_context, value_heads, preferred_element_type...  17.1 us
  transfers between devices with their start and end apart: 4, of which 3 were waited for; matrix products, arithmetic and copies ran while one was open for 6% of the time, Pallas kernels for 0%

profile of v1, /device:TPU:0, one launch (start us, length us, event | category | flops | bytes accessed | tf_op | source)
XLA Modules:
  0.0 437.2 jit_solution(2015930651248177552)
XLA Ops:
  7.3 0.9 copy.51
  8.4 0.7 broadcast_compare_fusion
  9.1 2.4 convolution_convert_fusion.6
  11.5 0.8 add_convert_fusion.6
  12.3 10.5 %fusion = (f32[6,1024]{1,0:T(8,128)S(1)}, f32[6,1024,1024]{1,2,0:T(8,128)}) fusion(pred[1024,1024]{0,1:T(8,128)(4,1)S(1)} %broadcast_compare_fusion, bf16[1024,6,64]{0,2,1:T(8,128)(2,1)S(1)} %bitcast.85, bf16[1024,6,64]{0,2,1:T(8,128)(2,1)S(1)} %bitcast.87), kind=kOutput, calls=%fused_computation.5 | convolution fusion | flops 824174592 | bytes 27811840 | tf_op jit(solution)/shard_map/qhd,khd->hqk/dot_general | solution.py:200
  22.9 11.3 %exponential_reduce_fusion = f32[6,1024]{1,0:T(8,128)S(1)} fusion(f32[6,1024,1024]{1,2,0:T(8,128)} %get-tuple-element.68, f32[6,1024]{1,0:T(8,128)S(1)} %is-finite_select_fusion, pred[1024,1024]{0,1:T(8,128)(4,1)S(1)} %broadcast_compare_fusion), kind=kLoop, calls=%fused_computation.3 | loop fusion | flops 25159680 | bytes 26263552 | tf_op jit(solution)/shard_map/reduce_sum | solution.py:247
  34.3 0.8 add_convert_fusion.7
  35.1 11.8 %convolution_convert_fusion.8 = bf16[6,64,1024]{2,1,0:T(8,128)(2,1)S(1)} fusion(bf16[1024,6,64]{0,2,1:T(8,128)(2,1)S(1)} %bitcast.95, f32[6,1024,1024]{1,2,0:T(8,128)} %get-tuple-element.68, f32[6,1024]{1,0:T(8,128)S(1)} %log_add_fusion, pred[1024,1024]{0,1:T(8,128)(4,1)S(1)} %broadcast_compare_fusion), kind=kOutput, calls=%fused_computation.67 | convolution fusion | flops 830865408 | bytes 27811840 | tf_op jit(solution)/shard_map/hqk,khd->qhd/dot_general | solution.py:249
  46.9 0.9 copy-done.42
  47.8 2.2 convolution_convert_fusion.2
  50.0 0.3 all-reduce.8.cloned.1.call-start
  50.3 22.9 %all-reduce.6.cloned.1.call-done = bf16[1024,768]{1,0:T(8,128)(2,1)} async-done(((bf16[1024,768]{1,0:T(8,128)(2,1)}), bf16[1024,768]{1,0:T(8,128)(2,1)}) %all-reduce.6.cloned.1.call-update) | async-done | bytes 1572880 | tf_op jit(solution)/shard_map/psum | solution.py:256
  73.3 2.6 fusion.11
  75.9 0.2 copy-done.5
  76.1 0.9 multiply_reduce_fusion.6
  77.0 17.9 %multiply_convert_fusion.1 = (bf16[1024,1536]{1,0:T(8,128)(2,1)S(1)}, f32[1024,1536]{1,0:T(8,128)}, f32[1024,1536]{1,0:T(8,128)}) fusion(f32[1536]{0:T(1024)S(1)} %copy-done.39, bf16[768,1536]{1,0:T(8,128)(2,1)S(1)} %copy-done, f32[768]{0:T(1024)S(1)} %copy-done.34, f32[768]{0:T(1024)S(1)} %copy-done.30, f32[1024]{0:T(1024)S(1)} %fusion.16, ...), kind=kOutput, calls=%fused_computation.11 | convolution fusion | flops 2526806016 | bytes 21257216 | tf_op jit(solution)/shard_map/dot_general | solution.py:264
  94.9 1.7 copy-done.46
  96.6 3.7 convolution_convert_fusion.4
  100.3 21.7 %all-reduce.8.cloned.1.call-done = bf16[1024,768]{1,0:T(8,128)(2,1)} async-done(((bf16[1024,768]{1,0:T(8,128)(2,1)}), bf16[1024,768]{1,0:T(8,128)(2,1)}) %all-reduce.8.cloned.1.call-update) | async-done | bytes 1572880 | tf_op jit(solution)/shard_map/psum | solution.py:267
  122.0 3.5 fusion.29
  125.6 0.5 multiply_reduce_fusion.5
  126.1 0.8 copy-done.13
  127.0 1.7 multiply_reduce_fusion.1
  128.7 2.8 fusion.28
  131.5 8.1 %convert_reduce_fusion = (f32[1536]{0:T(1024)S(1)}, bf16[1024,1536]{1,0:T(8,128)(2,1)S(1)}) fusion(f32[1024,1536]{1,0:T(8,128)S(1)} %bitcast.103, bf16[1536,768]{1,0:T(8,128)(2,1)S(1)} %copy-done.36, f32[1024,768]{1,0:T(8,128)S(1)} %get-tuple-element.41, f32[1024]{0:T(1024)S(1)} %negate_multiply_fusion.2, f32[1024,1536]{1,0:T(8,128)} %get-tuple-element.69, ...), kind=kOutput, calls=%fused_computation.9 | convolution fusion | flops 2444229120 | bytes 21250048 | tf_op jit(solution)/shard_map/dot_general | solution.py:193
  139.6 1.7 copy-done.44
  141.3 3.7 convolution_convert_fusion.3
  145.1 5.8 %convolution_convert_fusion.1 = bf16[1536,768]{1,0:T(8,128)(2,1)S(1)} fusion(bf16[1024,1536]{1,0:T(8,128)(2,1)} %copy-done.46, f32[1024,768]{1,0:T(8,128)} %copy-done.8, f32[1024]{0:T(1024)S(1)} %negate_multiply_fusion.2), kind=kOutput, calls=%fused_computation.28 | convolution fusion | flops 2418671616 | bytes 8654848 | tf_op jit(solution)/shard_map/dot_general | solution.py:187
  150.9 1.6 fusion.32
  152.5 0.6 copy-done.4
  153.1 0.7 copy-done.6
  153.7 12.1 %convolution_convert_fusion = bf16[768,1536]{1,0:T(8,128)(2,1)S(1)} fusion(bf16[1024,1536]{1,0:T(8,128)(2,1)S(1)} %copy-done.45, f32[768]{0:T(1024)S(1)} %copy-done.34, f32[768]{0:T(1024)S(1)} %copy-done.30, f32[1024]{0:T(1024)S(1)} %fusion.16, bf16[1024,768]{1,0:T(8,128)(2,1)S(1)} %copy-done.6, bf16[1024,768]{1,0:T(8,128)(2,1)S(1)} %copy-done.4, ...), kind=kOutput, calls=%fused_computation.27 | convolution fusion | flops 2424176640 | bytes 8668160 | tf_op jit(solution)/shard_map/dot_general | solution.py:187
  165.8 1.6 fusion.31
  167.4 4.7 %multiply_reduce_fusion.2 = (f32[768]{0:T(1024)S(1)}, f32[1024]{0:T(1024)S(1)}, f32[768]{0:T(1024)S(1)}, f32[768]{0:T(1024)S(1)}) fusion(f32[1024]{0:T(1024)S(1)} %fusion.16, bf16[1024,768]{1,0:T(8,128)(2,1)} %all-reduce.10.cloned.1.call-done, f32[1024,768]{1,0:T(8,128)} %copy-done.8, f32[1024]{0:T(1024)S(1)} %negate_multiply_fusion.2, ...), kind=kLoop, calls=%fused_computation.30 | loop fusion | flops 12579584 | bytes 7896064 | tf_op jit(solution)/shard_map/transpose(jvp())/reduce_sum | solution.py:179
  172.2 2.1 fusion.27
  174.3 1.6 copy-done.10
  175.9 0.9 convolution_convert_fusion.5
  176.9 0.9 copy-done.23
  177.7 12.6 %convert_reduce_fusion.1 = (f32[6,64]{1,0:T(8,128)S(1)}, bf16[6,64,1024]{2,1,0:T(8,128)(2,1)}) fusion(bf16[1024,6,64]{0,2,1:T(8,128)(2,1)S(1)} %bitcast.97, f32[6,1024,1024]{1,2,0:T(8,128)} %get-tuple-element.68, f32[6,1024]{1,0:T(8,128)S(1)} %log_add_fusion, pred[1024,1024]{0,1:T(8,128)(4,1)S(1)} %broadcast_compare_fusion), kind=kOutput, calls=%fused_computation.58 | convolution fusion | flops 831651456 | bytes 27813376 | tf_op jit(solution)/shard_map/hqk,qhd->khd/dot_general | solution.py:293
  190.3 17.1 %multiply_reduce_fusion = (f32[6,1024]{1,0:T(8,128)S(1)}, f32[6,1024,1024]{1,2,0:T(8,128)}) fusion(f32[6,1024,1024]{1,2,0:T(8,128)} %get-tuple-element.68, f32[6,1024]{1,0:T(8,128)S(1)} %log_add_fusion, pred[1024,1024]{0,1:T(8,128)(4,1)S(1)} %broadcast_compare_fusion, bf16[1024,6,64]{0,2,1:T(8,128)(2,1)} %bitcast.98, bf16[1024,6,64]{0,2,1:T(8,128)(2,1)S(1)} %bitcast.96), kind=kOutput, calls=%fused_computation.1 | convolution fusion | flops 836757504 | bytes 53002240 | tf_op jit(solution)/shard_map/qhd,khd->hqk/dot_general | solution.py:299
  207.4 21.7 %multiply_convert_fusion = bf16[6,1024,1024]{1,2,0:T(8,128)(2,1)} fusion(f32[6,1024,1024]{1,2,0:T(8,128)} %get-tuple-element.71, f32[6,1024,1024]{1,2,0:T(8,128)} %get-tuple-element.68, f32[6,1024]{1,0:T(8,128)S(1)} %get-tuple-element.70, f32[6,1024]{1,0:T(8,128)S(1)} %log_add_fusion, pred[1024,1024]{0,1:T(8,128)(4,1)S(1)} %broadcast_compare_fusion), kind=kLoop, calls=%fused_computation | loop fusion | flops 37748736 | bytes 64012288 | tf_op jit(solution)/shard_map/convert_element_type | solution.py:301
  229.1 8.6 %multiply_convert_fusion.2 = bf16[6,64,1024]{2,1,0:T(8,128)(2,1)S(1)} fusion(bf16[1024,6,64]{0,2,1:T(8,128)(2,1)S(1)} %bitcast.86, bf16[6,1024,1024]{1,2,0:T(8,128)(2,1)} %multiply_convert_fusion), kind=kOutput, calls=%fused_computation.60 | convolution fusion | flops 806092800 | bytes 14155776 | tf_op jit(solution)/shard_map/hqk,qhd->khd/dot_general | solution.py:312
  237.7 6.9 %convert_reduce_fusion.2 = (f32[6,64]{1,0:T(8,128)S(1)}, bf16[6,64,1024]{2,1,0:T(8,128)(2,1)S(1)}) fusion(bf16[1024,6,64]{0,2,1:T(8,128)(2,1)S(1)} %bitcast.88, bf16[6,1024,1024]{1,2,0:T(8,128)(2,1)} %multiply_convert_fusion), kind=kOutput, calls=%fused_computation.59 | convolution fusion | flops 806878848 | bytes 14157312 | tf_op jit(solution)/shard_map/hqk,khd->qhd/dot_general | solution.py:304
  244.7 1.8 fusion.13
  246.5 2.7 fusion.35
  249.4 2.2 fusion.36
  251.7 2.2 add_convert_fusion.2
  253.9 1.0 fusion.14
  255.0 1.1 pad_maximum_fusion.refs_4_
  256.1 0.3 copy-done.43
  256.4 0.9 convolution_convert_fusion.9
  257.6 1.0 fusion.15
  258.6 1.1 maximum_maximum_fusion.refs_5_
  259.7 15.9 %all-reduce.12.cloned.1.call-done = bf16[1024,768]{1,0:T(8,128)(2,1)} async-done(((bf16[1024,768]{1,0:T(8,128)(2,1)}), bf16[1024,768]{1,0:T(8,128)(2,1)}) %all-reduce.12.cloned.1.call-update) | async-done | bytes 1572880 | tf_op jit(solution)/shard_map/psum | solution.py:330
  275.7 4.0 add_reduce_fusion
  279.8 138.2 %sum_over_dp.1 = (bf16[768,768]{1,0:T(8,128)(2,1)S(1)}, bf16[768,768]{1,0:T(8,128)(2,1)S(1)}, bf16[768,768]{1,0:T(8,128)(2,1)S(1)}, bf16[768,768]{1,0:T(8,128)(2...) custom-call(bf16[768,768]{1,0:T(8,128)(2,1)} %get-tuple-element.52.refs_0_, ...), custom_call_target="tpu_custom_call" | custom-call | tf_op jit(solution)/shard_map/sum_over_dp/pallas_call | solution.py:161
  418.0 0.6 slice_bitcast_fusion.7
  418.6 0.6 slice_bitcast_fusion
  419.2 0.6 slice_bitcast_fusion.1
  419.8 1.1 fusion.33
  420.9 2.9 slice_convert_fusion.1
  423.8 1.1 maximum_convert_fusion.2
  424.9 2.8 maximum_convert_fusion
  427.7 2.5 maximum_convert_fusion.1
  (125 shorter events, 1.2 us)
Async XLA Ops:
  7.2 69.8 %copy-start = (bf16[768,1536]{1,0:T(8,128)(2,1)S(1)}, bf16[768,1536]{1,0:T(8,128)(2,1)}, u32[]{:S(2)}) copy-start(bf16[768,1536]{1,0:T(8,128)(2,1)} %param.30) | copy-start | bytes 7077892
  7.2 4.2 copy-start.40
  7.2 66.0 %all-reduce.6.cloned.1.call-start = ((), (), s32[]{:S(2)}) async-start(), calls=%async_computation | async-start | bytes 3145728 | tf_op jit(solution)/shard_map/psum | solution.py:256
  8.3 3.1 copy-start.2
  8.3 3.2 copy-start.24
  11.5 11.4 %copy-start.17 = (bf16[1024,384]{0,1:T(8,128)(2,1)}, bf16[1024,384]{0,1:T(8,128)(2,1)S(1)}, u32[]{:S(2)}) copy-start(bf16[1024,384]{0,1:T(8,128)(2,1)S(1)} %convolution_convert_fusion.6) | copy-start | bytes 2359300
  12.3 10.5 %copy-start.15 = (bf16[1024,384]{0,1:T(8,128)(2,1)}, bf16[1024,384]{0,1:T(8,128)(2,1)S(1)}, u32[]{:S(2)}) copy-start(bf16[1024,384]{0,1:T(8,128)(2,1)S(1)} %add_convert_fusion.6) | copy-start | bytes 2359300
  22.9 11.4 %copy-start.26 = (bf16[768,384]{1,0:T(8,128)(2,1)S(1)}, bf16[768,384]{1,0:T(8,128)(2,1)}, u32[]{:S(2)}) copy-start(bf16[768,384]{1,0:T(8,128)(2,1)} %param.24) | copy-start | bytes 1769476
  22.9 11.4 %copy-start.41 = (f32[384]{0:T(512)S(1)}, f32[384]{0:T(512)}, u32[]{:S(2)}) copy-start(f32[384]{0:T(512)} %param.25) | copy-start | bytes 4612
  35.1 11.8 %copy-start.21 = (bf16[1024,384]{0,1:T(8,128)(2,1)}, bf16[1024,384]{0,1:T(8,128)(2,1)S(1)}, u32[]{:S(2)}) copy-start(bf16[1024,384]{0,1:T(8,128)(2,1)S(1)} %add_convert_fusion.7) | copy-start | bytes 2359300
  35.1 12.7 %copy-start.37 = (bf16[384,768]{1,0:T(8,128)(2,1)S(1)}, bf16[384,768]{1,0:T(8,128)(2,1)}, u32[]{:S(2)}) copy-start(bf16[384,768]{1,0:T(8,128)(2,1)} %param.26) | copy-start | bytes 1769476
  46.9 0.9 copy-start.42
  46.9 26.3 %copy-start.29 = (f32[768]{0:T(1024)S(1)}, f32[768]{0:T(1024)}, u32[]{:S(2)}) copy-start(f32[768]{0:T(1024)} %param.27) | copy-start | bytes 9220
  50.0 27.0 %copy-start.30 = (f32[768]{0:T(1024)S(1)}, f32[768]{0:T(1024)}, u32[]{:S(2)}) copy-start(f32[768]{0:T(1024)} %param.28) | copy-start | bytes 9220
  50.0 27.0 %copy-start.34 = (f32[768]{0:T(1024)S(1)}, f32[768]{0:T(1024)}, u32[]{:S(2)}) copy-start(f32[768]{0:T(1024)} %param.29) | copy-start | bytes 9220
  50.0 27.0 %copy-start.39 = (f32[1536]{0:T(1024)S(1)}, f32[1536]{0:T(1024)}, u32[]{:S(2)}) copy-start(f32[1536]{0:T(1024)} %param.31) | copy-start | bytes 18436
  50.0 72.0 %all-reduce.8.cloned.1.call-start = ((), (), s32[]{:S(2)}) async-start(), calls=%async_computation.1 | async-start | bytes 3145728 | tf_op jit(solution)/shard_map/psum | solution.py:267
  73.2 2.6 copy-start.3
  73.3 2.8 copy-start.5
  77.0 19.6 %copy-start.35 = (bf16[1536,768]{1,0:T(8,128)(2,1)S(1)}, bf16[1536,768]{1,0:T(8,128)(2,1)}, u32[]{:S(2)}) copy-start(bf16[1536,768]{1,0:T(8,128)(2,1)} %param.32) | copy-start | bytes 7077892
  94.9 1.7 copy-start.46
  96.6 25.4 %copy-start.33 = (f32[768]{0:T(1024)S(1)}, f32[768]{0:T(1024)}, u32[]{:S(2)}) copy-start(f32[768]{0:T(1024)} %param.33) | copy-start | bytes 9220
  100.3 67.1 %all-reduce.10.cloned.1.call-start = ((), (), s32[]{:S(2)}) async-start(), calls=%async_computation.2 | async-start | bytes 3145728 | tf_op jit(solution)/shard_map/psum | solution.py:281
  122.0 9.5 %slice-start = ((s8[6291456]{0:T(1024)(128)(4,1)}), s8[4194304]{0:T(1024)(128)(4,1)S(1)}, s32[]{:S(2)}) async-start(s8[6291456]{0:T(1024)(128)(4,1)} %bitcast.102), calls=%async_computation.4 | async-start | bytes 8388608
  125.5 1.4 copy-start.13
  125.6 1.4 copy-start.31
  126.1 2.5 copy-start.32
  127.0 4.5 %slice-start.1 = ((s8[6291456]{0:T(1024)(128)(4,1)}), s8[2097152]{0:T(1024)(128)(4,1)S(1)}, s32[]{:S(2)}) async-start(s8[6291456]{0:T(1024)(128)(4,1)} %bitcast.102), calls=%async_computation.5 | async-start | bytes 4194304
  128.7 2.8 copy-start.36
  131.4 8.1 %copy-start.8 = (f32[1024,768]{1,0:T(8,128)}, f32[1024,768]{1,0:T(8,128)S(1)}, u32[]{:S(2)}) copy-start(f32[1024,768]{1,0:T(8,128)S(1)} %get-tuple-element.41) | copy-start | bytes 9437188
  139.6 1.8 copy-start.44
  145.1 130.6 %all-reduce.12.cloned.1.call-start = ((), (), s32[]{:S(2)}) async-start(), calls=%async_computation.3 | async-start | bytes 3145728 | tf_op jit(solution)/shard_map/psum | solution.py:330
  145.1 7.4 %copy-start.45 = (bf16[1024,1536]{1,0:T(8,128)(2,1)S(1)}, bf16[1024,1536]{1,0:T(8,128)(2,1)}, u32[]{:S(2)}) copy-start(bf16[1024,1536]{1,0:T(8,128)(2,1)} %copy-done.44) | copy-start | bytes 9437188
  150.9 2.2 copy-start.4
  150.9 2.8 copy-start.6
  167.4 4.8 %copy-start.7 = (bf16[1024,768]{1,0:T(8,128)(2,1)S(1)}, bf16[1024,768]{1,0:T(8,128)(2,1)}, u32[]{:S(2)}) copy-start(bf16[1024,768]{1,0:T(8,128)(2,1)} %all-reduce.6.cloned.1.call-done) | copy-start | bytes 4718596
  167.4 4.8 %copy-start.9 = (f32[1024,768]{1,0:T(8,128)S(1)}, f32[1024,768]{1,0:T(8,128)}, u32[]{:S(2)}) copy-start(f32[1024,768]{1,0:T(8,128)} %copy-done.8) | copy-start | bytes 9437188
  167.4 4.8 %copy-start.14 = (bf16[1024,768]{1,0:T(8,128)(2,1)S(1)}, bf16[1024,768]{1,0:T(8,128)(2,1)}, u32[]{:S(2)}) copy-start(bf16[1024,768]{1,0:T(8,128)(2,1)} %all-reduce.10.cloned.1.call-done) | copy-start | bytes 4718596
  172.2 3.7 copy-start.38
  174.2 1.7 copy-start.10
  176.8 0.9 copy-start.23
  177.7 12.6 %copy-start.22 = (bf16[1024,384]{0,1:T(8,128)(2,1)S(1)}, bf16[1024,384]{0,1:T(8,128)(2,1)}, u32[]{:S(2)}) copy-start(bf16[1024,384]{0,1:T(8,128)(2,1)} %copy-done.21) | copy-start | bytes 2359300
  207.4 21.7 %copy-start.16 = (bf16[1024,384]{0,1:T(8,128)(2,1)S(1)}, bf16[1024,384]{0,1:T(8,128)(2,1)}, u32[]{:S(2)}) copy-start(bf16[1024,384]{0,1:T(8,128)(2,1)} %copy-done.15) | copy-start | bytes 2359300
  229.1 8.6 %copy-start.18 = (bf16[1024,384]{0,1:T(8,128)(2,1)S(1)}, bf16[1024,384]{0,1:T(8,128)(2,1)}, u32[]{:S(2)}) copy-start(bf16[1024,384]{0,1:T(8,128)(2,1)} %copy-done.17) | copy-start | bytes 2359300
  244.7 1.9 copy-start.25
  249.2 2.4 copy-start.19
  249.4 2.2 copy-start.12
  249.4 2.3 copy-start.27
  253.9 1.1 copy-start.28
  253.9 2.2 copy-start.11
  253.9 2.5 copy-start.43
  256.4 1.1 copy-start.20
  427.7 2.5 copy-start.1
Sparse Core Ops, SparseCore 0:
  50.1 23.0 all-reduce.5
  100.4 21.5 all-reduce.7
  145.2 21.5 all-reduce.9
  254.0 21.6 all-reduce.11

commit v2 on v1

v2 whole, which is shorter than its diff:
```python
import functools
import math

import jax
import jax.numpy as jnp
from jax import lax
from jax.experimental import pallas as pl
from jax.experimental.pallas import tpu as pltpu
from jax.sharding import PartitionSpec as P

HEAD_DIM = 64
PAIR = 2 * HEAD_DIM
LONGEST = 200
BLOCK = 256
STRIP = 32
MESH = pl.DeviceIdType.MESH


EPSILON = 1e-12
NEGATIVE = -1e30
ROW_TILE = 16


def bits_of(count):
    bits, stride = [], 1
    while stride < count:
        bits.append(stride)
        stride *= 2
    return bits


def exchange_orders(count):
    bits = bits_of(count)
    if len(bits) < 3:
        return [bits, bits[::-1]]
    return [[bits[0], bits[2], bits[1]] + bits[3:], [bits[1], bits[2], bits[0]] + bits[3:]]


def plan_steps(rows, order):
    halvings, wholes, length = [], [], rows
    for stride in order:
        if (length // 2) % ROW_TILE == 0 and length % 2 == 0:
            length //= 2
            halvings.append((stride, length, "halve"))
        else:
            wholes.append((stride, length, "whole"))
    gathers = [(stride, sent, "gather") for stride, sent, _ in reversed(halvings)]
    return halvings + wholes + gathers


def landing_rows(steps):
    return sum(sent for _, sent, kind in steps if kind != "gather")


class Reduction:
    def __init__(self, block, total, landing, send_sem, recv_sem, steps, dp, mp):
        self.total, self.landing, self.send_sem, self.recv_sem = total, landing, send_sem, recv_sem
        self.steps, self.dp, self.mp = steps, dp, mp
        self.held, self.base = block, 0
        self.low, self.offset = 0, 0
        self.copies, self.next_step = [], 0

    def side(self, stride):
        return (self.dp // stride) % 2

    def advance(self):
        step = self.next_step
        if step > 0:
            self.finish(step - 1)
        if step < len(self.steps):
            self.start(step)
        self.next_step += 1

    def start(self, step):
        stride, sent, kind = self.steps[step]
        side = self.side(stride)
        if kind == "gather":
            rows = pl.ds(pl.multiple_of(self.low, ROW_TILE), sent)
            source, target = self.total.at[rows], self.total.at[rows]
        else:
            start = self.base + (1 - side) * sent if kind == "halve" else self.base
            source = self.held.at[pl.ds(pl.multiple_of(start, ROW_TILE), sent)]
            target = self.landing.at[pl.ds(self.offset, sent)]
        copy = pltpu.make_async_remote_copy(
            source,
            target,
            self.send_sem.at[step],
            self.recv_sem.at[step],
            device_id=(self.dp + stride - 2 * stride * side, self.mp),
            device_id_type=MESH,
        )
        copy.start()
        self.copies.append(copy)

    def finish(self, step):
        stride, sent, kind = self.steps[step]
        side = self.side(stride)
        self.copies[step].wait()
        if kind == "gather":
            self.low = self.low - side * sent
            return
        kept = self.base + side * sent if kind == "halve" else self.base
        if kind == "halve":
            self.low = self.low + side * sent
        last = step + 1 == len(self.steps) or (
            self.steps[step + 1][2] == "gather"
        )
        held, offset, low = self.held, self.offset, self.low
        part = sent
        while part > 64 and part % 2 == 0 and (part // 2) % ROW_TILE == 0:
            part //= 2

        def add(index, carry):
            own = pl.ds(pl.multiple_of(kept + index * part, ROW_TILE), part)
            came = pl.ds(pl.multiple_of(offset + index * part, ROW_TILE), part)
            both = held[own].astype(jnp.float32) + self.landing[came].astype(jnp.float32)
            if last:
                done = pl.ds(pl.multiple_of(low + index * part, ROW_TILE), part)
                self.total[done] = both.astype(self.total.dtype)
            else:
                self.landing[came] = both.astype(self.landing.dtype)
            return carry

        lax.fori_loop(0, sent // part, add, 0)
        self.held, self.base = self.landing, offset
        self.offset += sent


def dot(left, right, left_dim, right_dim):
    return lax.dot_general(
        left, right, (((left_dim,), (right_dim,)), ((), ())), preferred_element_type=jnp.float32
    )


def column_sums(values):
    return jnp.sum(values.reshape(values.shape[0] // 8, 8, values.shape[1]), axis=0)


def key_window(block, row_count):
    low = max(0, (block * BLOCK - (LONGEST - 1)) // 128 * 128)
    high = min(row_count, -(-((block + 1) * BLOCK + LONGEST - 1) // 128) * 128)
    return low, high


def layer_kernel(
    plans,
    vector_plan,
    strides,
    tokens_hbm,
    cotangent_hbm,
    lengths,
    query_weight_hbm,
    key_weight_hbm,
    value_weight_hbm,
    output_weight_hbm,
    up_weight_hbm,
    down_weight_hbm,
    query_bias,
    value_bias,
    output_bias,
    first_gain,
    first_shift,
    up_bias,
    down_bias,
    second_gain,
    second_shift,
    result_hbm,
    tokens_grad_hbm,
    *refs,
):
    count = len(plans)
    totals, vector_total = refs[:count], refs[count]
    (
        tokens,
        cotangent,
        qkv_weight,
        output_weight,
        up_weight,
        down_weight,
        qkv,
        context,
        log_totals,
        segment_row,
        segment_column,
        parts,
        landed,
        first_hat,
        first_scale,
        first_low,
        slope,
        inner,
        d_pre,
        d_resid,
        grad_low,
        down_blocks,
        up_blocks,
        vector_sums,
        up_bias_sums,
        vectors,
        block_landings,
        vector_landing,
        load_sem,
        store_sem,
        part_send,
        part_recv,
        chain_send,
        chain_recv,
        vector_send,
        vector_recv,
    ) = refs[count + 1 :]
    row_count, width = tokens.shape
    shard = context.shape[1]
    hidden = inner.shape[1]
    blocks = row_count // BLOCK
    strips = BLOCK // STRIP
    pairs = shard // PAIR
    dp, mp = lax.axis_index("dp"), lax.axis_index("mp")
    other = 1 - mp

    barrier = pltpu.get_barrier_semaphore()
    for stride in strides:
        partner = dp + stride - 2 * stride * ((dp // stride) % 2)
        pl.semaphore_signal(barrier, inc=1, device_id=(partner, mp), device_id_type=MESH)
    pl.semaphore_signal(barrier, inc=1, device_id=(dp, other), device_id_type=MESH)

    loads = [
        pltpu.make_async_copy(source, target, load_sem.at[i])
        for i, (source, target) in enumerate(
            [
                (tokens_hbm, tokens),
                (query_weight_hbm, qkv_weight.at[:, :shard]),
                (key_weight_hbm, qkv_weight.at[:, shard : 2 * shard]),
                (value_weight_hbm, qkv_weight.at[:, 2 * shard :]),
                (output_weight_hbm, output_weight),
                (up_weight_hbm, up_weight),
                (down_weight_hbm, down_weight),
                (cotangent_hbm, cotangent),
            ]
        )
    ]
    for copy in loads:
        copy.start()

    runs = lengths.shape[1]
    row_place = lax.broadcasted_iota(jnp.int32, (1, row_count), 1)
    column_place = lax.broadcasted_iota(jnp.int32, (row_count, 1), 0)
    in_row, in_column = jnp.zeros_like(row_place), jnp.zeros_like(column_place)
    end = 0
    for run in range(runs):
        end = end + lengths[0, run]
        in_row = in_row + (row_place >= end).astype(jnp.int32)
        in_column = in_column + (column_place >= end).astype(jnp.int32)
    segment_row[...] = in_row
    segment_column[...] = in_column
    vector_sums[...] = jnp.zeros_like(vector_sums)
    up_bias_sums[...] = jnp.zeros_like(up_bias_sums)
    vectors[...] = jnp.zeros_like(vectors)

    head_lanes = lax.broadcasted_iota(jnp.int32, (1, PAIR), 1) < HEAD_DIM
    keep_head = [
        head_lanes.astype(jnp.float32).astype(jnp.bfloat16),
        (1.0 - head_lanes.astype(jnp.float32)).astype(jnp.bfloat16),
    ]

    def rows_of(block):
        return pl.ds(pl.multiple_of(block * BLOCK, BLOCK), BLOCK)

    def strip_of(block, strip):
        return pl.ds(pl.multiple_of(block * BLOCK + strip * STRIP, STRIP), STRIP)

    def part_copy(turn, block):
        rows = rows_of(block)
        return pltpu.make_async_remote_copy(
            parts.at[turn % 2, rows],
            landed.at[turn % 2, rows],
            part_send.at[turn, block],
            part_recv.at[turn, block],
            device_id=(dp, other),
            device_id_type=MESH,
        )

    def both_parts(turn, rows):
        return parts[turn % 2, rows, :].astype(jnp.float32) + landed[turn % 2, rows, :].astype(
            jnp.float32
        )

    def send_part(turn, block, value):
        if turn >= 2:
            part_copy(turn - 2, block).wait_send()
        parts[turn % 2, rows_of(block), :] = value.astype(jnp.bfloat16)
        part_copy(turn, block).start()

    def each(number, body, unroll=1):
        lax.fori_loop(0, number, lambda i, carry: (body(i), carry)[1], 0, unroll=unroll)

    def add_vector(place, values):
        vector_sums[place] = vector_sums[place] + column_sums(values)

    for copy in loads[:4]:
        copy.wait()
    scale = 1.0 / math.sqrt(HEAD_DIM)

    def project(block):
        rows = rows_of(block)
        got = dot(tokens[rows, :], qkv_weight[...], 1, 0)
        qkv[rows, :shard] = ((got[:, :shard] + query_bias[...]) * scale).astype(jnp.bfloat16)
        qkv[rows, shard : 2 * shard] = got[:, shard : 2 * shard].astype(jnp.bfloat16)
        qkv[rows, 2 * shard :] = (got[:, 2 * shard :] + value_bias[...]).astype(jnp.bfloat16)

    for block in range(blocks):
        project(block)

    def pair_inputs(block, pair):
        low, high = key_window(block, row_count)
        rows = pl.ds(block * BLOCK, BLOCK)
        keys = pl.ds(low, high - low)
        at = lambda group: pl.ds(pl.multiple_of(group * shard + pair * PAIR, PAIR), PAIR)
        bias = jnp.where(segment_column[keys, :] == segment_row[:, rows], 0.0, NEGATIVE)
        return rows, keys, qkv[rows, at(0)], qkv[keys, at(1)], qkv[keys, at(2)], bias, at

    def attend(block, pair):
        rows, keys, query, key, value, bias, at = pair_inputs(block, pair)
        outs = []
        for head in range(2):
            scores = dot(key, query * keep_head[head], 1, 1) + bias
            top = jnp.max(scores, axis=0, keepdims=True)
            raised = jnp.exp(scores - top)
            total = jnp.sum(raised, axis=0, keepdims=True)
            log_totals[2 * pair + head, :, rows] = top + jnp.log(total)
            weights = (raised * (1.0 / total)).astype(jnp.bfloat16)
            outs.append(dot(weights, value, 0, 0))
        context[rows, at(0)] = jnp.where(head_lanes, outs[0], outs[1]).astype(jnp.bfloat16)

    for copy in loads[4:]:
        copy.wait()
    for block in range(blocks):
        each(pairs, functools.partial(attend, block))
        if block == 0:
            pl.semaphore_wait(barrier, len(strides) + 1)
        send_part(0, block, dot(context[rows_of(block), :], output_weight[...], 1, 0))

    def normalized(values):
        centered = values - jnp.mean(values, axis=-1, keepdims=True)
        variance = jnp.mean(centered * centered, axis=-1, keepdims=True)
        inverse = lax.rsqrt(variance + EPSILON)
        return centered * inverse, inverse

    def pull_norm(grad, hat, inverse):
        return inverse * (
            grad
            - jnp.mean(grad, axis=-1, keepdims=True)
            - hat * jnp.mean(grad * hat, axis=-1, keepdims=True)
        )

    def feed_forward(block):
        part_copy(0, block).wait_recv()

        def norm(strip):
            rows = strip_of(block, strip)
            hat, inverse = normalized(
                tokens[rows, :].astype(jnp.float32) + both_parts(0, rows) + output_bias[...]
            )
            first_hat[rows, :] = hat
            first_scale[rows, :] = inverse
            first_low[rows, :] = (hat * first_gain[...] + first_shift[...]).astype(jnp.bfloat16)

        each(strips, norm, 2)
        rows = rows_of(block)
        tile = hidden // 4
        for start in range(0, hidden, tile):
            some = slice(start, start + tile)
            pre = dot(first_low[rows, :], up_weight[:, some], 1, 0) + up_bias[:, some]
            below = 0.5 + 0.5 * lax.erf(pre * math.sqrt(0.5))
            density = jnp.exp(-0.5 * pre * pre) * (1.0 / math.sqrt(2.0 * math.pi))
            inner[rows, some] = (pre * below).astype(jnp.bfloat16)
            slope[rows, some] = (below + pre * density).astype(jnp.bfloat16)
        send_part(1, block, dot(inner[rows, :], down_weight[...], 1, 0))

    each(blocks, feed_forward)

    def second_norm(block):
        part_copy(1, block).wait_recv()

        def norm(strip):
            rows = strip_of(block, strip)
            first = first_hat[rows, :] * first_gain[...] + first_shift[...]
            hat, inverse = normalized(first + both_parts(1, rows) + down_bias[...])
            live = (segment_column[rows, :] < runs - 1).astype(jnp.float32)
            grad = cotangent[rows, :].astype(jnp.float32) * live
            cotangent[rows, :] = (hat * second_gain[...] + second_shift[...]).astype(jnp.bfloat16)
            back = pull_norm(grad * second_gain[...], hat, inverse)
            d_resid[rows, :] = back
            grad_low[rows, :] = back.astype(jnp.bfloat16)
            add_vector(4, grad * hat)
            add_vector(5, grad)
            add_vector(3, back)

        each(strips, norm, 2)

    each(blocks, second_norm)
    result_store = pltpu.make_async_copy(cotangent, result_hbm, store_sem.at[0])
    result_store.start()

    at_attention = lambda place: inner.at[:width, place * width : (place + 1) * width]
    sources = [down_blocks.at[0], down_blocks.at[1], up_blocks.at[0], up_blocks.at[1]]
    sources += [at_attention(0), at_attention(1)]
    chains = [
        Reduction(
            sources[c],
            totals[c],
            block_landings.at[c],
            chain_send.at[c],
            chain_recv.at[c],
            plans[c],
            dp,
            mp,
        )
        for c in range(count)
    ]
    vector_chain = Reduction(
        vectors, vector_total, vector_landing, vector_send, vector_recv, vector_plan, dp, mp
    )

    def advance(*which):
        for c in which:
            (vector_chain if c == count else chains[c]).advance()

    half = width // 2
    for place in range(2):
        for start in range(0, width, half):
            some = slice(place * width + start, place * width + start + half)
            down_blocks[place, start : start + half, :] = dot(
                inner[:, some], grad_low[...], 0, 0
            ).astype(jnp.bfloat16)
        advance(place)

    def through_hidden(block):
        rows = rows_of(block)
        tile = hidden // 4
        for start in range(0, hidden, tile):
            some = slice(start, start + tile)
            grad = dot(grad_low[rows, :], down_weight[some, :], 1, 1)
            low = (grad * slope[rows, some].astype(jnp.float32)).astype(jnp.bfloat16)
            d_pre[rows, some] = low
            up_bias_sums[:, some] = up_bias_sums[:, some] + column_sums(low.astype(jnp.float32))
        send_part(2, block, dot(d_pre[rows, :], up_weight[...], 1, 1))

    each(blocks, through_hidden)

    for place in range(2):
        some = slice(place * width, (place + 1) * width)
        for start in range(0, width, half):
            up_blocks[place, start : start + half, :] = dot(
                first_low[:, start : start + half], d_pre[:, some], 0, 0
            ).astype(jnp.bfloat16)
        advance(2 + place)

    def first_norm_back(block):
        part_copy(2, block).wait_recv()

        def norm(strip):
            rows = strip_of(block, strip)
            grad = d_resid[rows, :] + both_parts(2, rows)
            hat = first_hat[rows, :]
            back = pull_norm(grad * first_gain[...], hat, first_scale[rows, :])
            d_resid[rows, :] = back
            grad_low[rows, :] = back.astype(jnp.bfloat16)
            add_vector(1, grad * hat)
            add_vector(2, grad)
            add_vector(0, back)

        each(strips, norm, 2)
        rows = rows_of(block)
        d_pre[rows, :shard] = dot(grad_low[rows, :], output_weight[...], 1, 1).astype(jnp.bfloat16)

    each(blocks, first_norm_back)

    for start in range(0, width, shard):
        inner[start : start + shard, width + shard : 2 * width] = dot(
            context[...], grad_low[:, start : start + shard], 0, 0
        ).astype(jnp.bfloat16)

    first_hat[...] = jnp.zeros_like(first_hat)

    def attend_back(block, pair):
        rows, keys, query, key, value, bias, at = pair_inputs(block, pair)
        d_context = d_pre[rows, at(0)]
        d_key = d_value = 0.0
        d_query = []
        for head in range(2):
            own_query, own_grad = query * keep_head[head], d_context * keep_head[head]
            scores = dot(key, own_query, 1, 1) + bias
            weights = jnp.exp(scores - log_totals[2 * pair + head, :, rows])
            d_weights = dot(value, own_grad, 1, 1)
            mean = jnp.sum(weights * d_weights, axis=0, keepdims=True)
            d_scores = (weights * (d_weights - mean)).astype(jnp.bfloat16)
            d_value = d_value + dot(weights.astype(jnp.bfloat16), own_grad, 1, 0)
            d_key = d_key + dot(d_scores, own_query, 1, 0)
            d_query.append(dot(d_scores, key, 0, 0))
        slope[rows, at(0)] = (jnp.where(head_lanes, d_query[0], d_query[1]) * scale).astype(
            jnp.bfloat16
        )
        first_hat[keys, at(0)] = first_hat[keys, at(0)] + d_key
        first_hat[keys, at(1)] = first_hat[keys, at(1)] + d_value

    for block in range(blocks):
        each(pairs, functools.partial(attend_back, block))
        advance(*PUMP_ATTEND[block])

    def round_keys(strip):
        rows = pl.ds(pl.multiple_of(strip * STRIP, STRIP), STRIP)
        slope[rows, shard : 3 * shard] = first_hat[rows, :].astype(jnp.bfloat16)

    each(row_count // STRIP, round_keys, 4)

    for start in range(0, width, half):
        inner[start : start + half, :width] = dot(
            tokens[:, start : start + half], slope[:, :width], 0, 0
        ).astype(jnp.bfloat16)
    advance(4)
    inner[:width, width : width + shard] = dot(
        tokens[...], slope[:, width : width + shard], 0, 0
    ).astype(jnp.bfloat16)
    advance(5)

    def finish_vectors():
        for place in range(6):
            vectors[place : place + 1, :] = jnp.sum(vector_sums[place], axis=0, keepdims=True)
        up_sum = jnp.sum(up_bias_sums[...], axis=0, keepdims=True)
        for place in range(hidden // width):
            vectors[6 + place : 7 + place, :] = up_sum[:, place * width : (place + 1) * width]
        ones = jnp.ones((16, row_count), jnp.bfloat16)
        last = 6 + hidden // width
        vectors[last : last + 1, :shard] = dot(ones, slope[:, :shard], 1, 0)[:1]
        vectors[last : last + 1, shard:] = dot(ones, slope[:, 2 * shard : 3 * shard], 1, 0)[:1]

    finish_vectors()
    advance(count)

    def token_part(block):
        rows = rows_of(block)
        send_part(3, block, dot(slope[rows, : 3 * shard], qkv_weight[...], 1, 1))

    for block in range(blocks):
        token_part(block)
        advance(*PUMP_TOKENS[block])

    def tokens_back(block):
        part_copy(3, block).wait_recv()

        def total(strip):
            rows = strip_of(block, strip)
            tokens[rows, :] = (d_resid[rows, :] + both_parts(3, rows)).astype(jnp.bfloat16)

        each(strips, total, 2)

    each(blocks, tokens_back)
    tokens_store = pltpu.make_async_copy(tokens, tokens_grad_hbm, store_sem.at[1])
    tokens_store.start()

    left = chains + [vector_chain]
    for chain_order in TAIL_ORDER(left):
        chain_order.advance()

    for turn in (2, 3):
        for block in range(blocks):
            part_copy(turn, block).wait_send()
    result_store.wait()
    tokens_store.wait()


PUMP_ATTEND = [(0, 1), (), (0, 1, 2, 3), ()]
PUMP_TOKENS = [(), (), (), ()]


def TAIL_ORDER(chains):
    remaining = {i: len(c.steps) + 1 - c.next_step for i, c in enumerate(chains)}
    order = []
    while any(remaining.values()):
        for i, c in enumerate(chains):
            if remaining[i]:
                order.append(c)
                remaining[i] -= 1
    return order


def local(
    tokens,
    cotangent,
    lengths,
    query_weight,
    query_bias,
    key_weight,
    value_weight,
    value_bias,
    output_weight,
    output_bias,
    first_gain,
    first_shift,
    up_weight,
    up_bias,
    down_weight,
    down_bias,
    second_gain,
    second_shift,
):
    row_count, width = tokens.shape
    shard, hidden = query_weight.shape[1], up_weight.shape[1]
    dp_size = lax.axis_size("dp")
    blocks = row_count // BLOCK
    low, wide = jnp.bfloat16, jnp.float32
    count = 6
    orders = exchange_orders(dp_size)
    plans = [plan_steps(width, orders[i % 2]) for i in range(count)]
    vector_rows = ROW_TILE
    vector_plan = [(stride, vector_rows, "whole") for stride in orders[0]]
    landing = max(landing_rows(plan) for plan in plans)
    steps = max(len(plan) for plan in plans)
    hbm = pl.BlockSpec(memory_space=pl.ANY)
    vmem = pl.BlockSpec(memory_space=pltpu.VMEM)
    smem = pl.BlockSpec(memory_space=pltpu.SMEM)
    dma = pltpu.SemaphoreType.DMA
    flat = lambda v: v.reshape(1, -1)
    outs = pl.pallas_call(
        functools.partial(layer_kernel, plans, vector_plan, bits_of(dp_size)),
        out_shape=[
            jax.ShapeDtypeStruct((row_count, width), low),
            jax.ShapeDtypeStruct((row_count, width), low),
            *[jax.ShapeDtypeStruct((width, width), low)] * count,
            jax.ShapeDtypeStruct((vector_rows, width), wide),
        ],
        in_specs=[hbm, hbm, smem] + [hbm] * 6 + [vmem] * 9,
        out_specs=[hbm, hbm] + [vmem] * (count + 1),
        scratch_shapes=[
            pltpu.VMEM((row_count, width), low),
            pltpu.VMEM((row_count, width), low),
            pltpu.VMEM((width, 3 * shard), low),
            pltpu.VMEM((shard, width), low),
            pltpu.VMEM((width, hidden), low),
            pltpu.VMEM((hidden, width), low),
            pltpu.VMEM((row_count, 3 * shard), low),
            pltpu.VMEM((row_count, shard), low),
            pltpu.VMEM((shard // HEAD_DIM, 1, row_count), wide),
            pltpu.VMEM((1, row_count), jnp.int32),
            pltpu.VMEM((row_count, 1), jnp.int32),
            pltpu.VMEM((2, row_count, width), low),
            pltpu.VMEM((2, row_count, width), low),
            pltpu.VMEM((row_count, width), wide),
            pltpu.VMEM((row_count, 1), wide),
            pltpu.VMEM((row_count, width), low),
            pltpu.VMEM((row_count, hidden), low),
            pltpu.VMEM((row_count, hidden), low),
            pltpu.VMEM((row_count, hidden), low),
            pltpu.VMEM((row_count, width), wide),
            pltpu.VMEM((row_count, width), low),
            pltpu.VMEM((2, width, width), low),
            pltpu.VMEM((2, width, width), low),
            pltpu.VMEM((6, 8, width), wide),
            pltpu.VMEM((8, hidden), wide),
            pltpu.VMEM((vector_rows, width), wide),
            pltpu.VMEM((count, landing, width), low),
            pltpu.VMEM((max(1, len(vector_plan)) * vector_rows, width), wide),
            dma((8,)),
            dma((2,)),
            dma((4, blocks)),
            dma((4, blocks)),
            dma((count, steps)),
            dma((count, steps)),
            dma((max(1, len(vector_plan)),)),
            dma((max(1, len(vector_plan)),)),
        ],
        compiler_params=pltpu.CompilerParams(
            collective_id=0, has_side_effects=True, vmem_limit_bytes=63 * 2**20
        ),
        name="layer",
    )(
        tokens,
        cotangent,
        lengths,
        query_weight,
        key_weight,
        value_weight,
        output_weight,
        up_weight,
        down_weight,
        flat(query_bias),
        flat(value_bias),
        flat(output_bias),
        flat(first_gain),
        flat(first_shift),
        flat(up_bias),
        flat(down_bias),
        flat(second_gain),
        flat(second_shift),
    )
    result, tokens_grad, down_top, down_bottom, up_left, up_right, query_key, value_output, sums = (
        outs
    )
    f32 = lambda total: total.astype(jnp.float32)
    return (
        result,
        tokens_grad,
        f32(query_key[:, :shard]),
        sums[8, :shard],
        f32(query_key[:, shard:]),
        f32(value_output[:, :shard]),
        sums[8, shard:],
        f32(jnp.concatenate([value_output[:shard, shard:], value_output[shard:, shard:]], axis=1)),
        sums[0],
        sums[1],
        sums[2],
        f32(jnp.concatenate([up_left, up_right], axis=1)),
        sums[6:8].reshape(-1),
        f32(jnp.concatenate([down_top, down_bottom], axis=0)),
        sums[3],
        sums[4],
        sums[5],
    )


def solution(mesh):
    in_specs = (
        P("dp", None),
        P("dp", None),
        P("dp", None),
        P(None, "mp"),
        P("mp"),
        P(None, "mp"),
        P(None, "mp"),
        P("mp"),
        P("mp", None),
        P(),
        P(),
        P(),
        P(None, "mp"),
        P("mp"),
        P("mp", None),
        P(),
        P(),
        P(),
    )
    out_specs = (
        P("dp", None),
        P("dp", None),
        P(None, "mp"),
        P("mp"),
        P(None, "mp"),
        P(None, "mp"),
        P("mp"),
        P("mp", None),
        P(),
        P(),
        P(),
        P(None, "mp"),
        P("mp"),
        P("mp", None),
        P(),
        P(),
        P(),
    )
    return jax.shard_map(local, mesh=mesh, in_specs=in_specs, out_specs=out_specs, check_vma=False)
```

time: 445 us -> 231 us (0.52); the launches traced: 437 us -> 230 us
  matrix products: 138 us -> 0 us
  Pallas kernels: 138 us -> 199 us
  waiting for transfers between devices: 60.6 us -> 0 us
  other arithmetic: 68.4 us -> 8.34 us
  between operations: 14.9 us -> 0.69 us
  local copies, waits for them, and re-layouts: 17 us -> 21.7 us
    dot_general x24 -> x0, matrix products: 138 us -> none  [the longest x6 22.7 us: contract_rows(): lax.dot_general(left, right, (((0,), (0,)), ((), ())), preferred_element_...]
    pallas_call x1, Pallas kernels: 138 us -> 199 us  [local(): pl.pallas_call(functools.partial(layer_kernel, plans, vector_plan, bits_o...]
    psum x4 -> x0, waiting for transfers between devices: 60.5 us -> none  [the longest x1 22.9 us: local(): lax.psum(jnp.dot(context, output_weight, preferred_element_type=jnp.float...]
    reduce_sum x11 -> x0, other arithmetic: 34.2 us -> none  [the longest x1 11.3 us: local(): log_total = jax.nn.logsumexp(scores, axis=-1, keepdims=True)]
    convert_element_type x3 -> x4, other arithmetic: 24.6 us -> 8.34 us  [local(): f32 = lambda total: total.astype(jnp.float32)]
    reshape x1 -> x10, local copies, waits for them, and re-layouts: 0.01 us -> 12 us  [the longest x9 11.4 us: local(): flat = lambda v: v.reshape(1, -1)]
    concatenate x5 -> x0, other arithmetic: 8.68 us -> none  [the longest x1 2.82 us: local(): up_weight_grad = jnp.concatenate([wide(blocks[2]), wide(blocks[3])], axis=1)]
    unnamed x106 -> x18, local copies, waits for them, and re-layouts: 9.87 us -> 4.81 us
  transfers between devices with their start and end apart: 4 -> 0, of which waited for: 3 -> 0; matrix products, arithmetic and copies ran while one was open for 6% -> 0% of each run, Pallas kernels for 0% -> 0%
where the time goes in v2:
time: 231 us; the launch traced here: 230 us
  Pallas kernels  199 us (86%)
  local copies, waits for them, and re-layouts  21.7 us (9%)
  other arithmetic  8.34 us (4%)
    pallas_call x1, Pallas kernels, local(): pl.pallas_call(functools.partial(layer_kernel, plans, vector_plan, bits_o...  199 us
    reshape x9, local copies, waits for them, and re-layouts, local(): flat = lambda v: v.reshape(1, -1)  11.4 us
    convert_element_type x4, other arithmetic, local(): f32 = lambda total: total.astype(jnp.float32)  8.34 us
    unnamed x18, local copies, waits for them, and re-layouts  4.81 us

profile of v2, /device:TPU:0, one launch (start us, length us, event | category | flops | bytes accessed | tf_op | source)
XLA Modules:
  0.0 229.9 jit_solution(11183778471826326415)
XLA Ops:
  0.7 1.2 reshape.64.query_bias
  1.9 1.2 reshape.65.value_bias
  3.1 1.3 reshape.66.output_bias
  4.4 1.3 reshape.67.first_gain
  5.7 1.3 reshape.68.first_shift
  6.9 1.3 reshape.70.down_bias
  8.2 1.3 reshape.71.second_gain
  9.5 1.3 reshape.72.second_shift
  10.7 1.3 reshape.69.up_bias
  12.0 199.2 %layer.1 = (bf16[1024,768]{1,0:T(8,128)(2,1)}, bf16[1024,768]{1,0:T(8,128)(2,1)}, bf16[768,768]{1,0:T(8,128)(2,1)}, bf16[768,768]{1,0:T(8,128)(2,1)}, bf16[768,7...) custom-call(bf16[1024,768]{1,0:T(8,128)(2,1)} %tokens_hbm.1, ...), custom_call_target="tpu_custom_call" | custom-call | tf_op jit(solution)/shard_map/layer/pallas_call | solution.py:624
  211.2 1.3 slice_reduce_fusion.6
  212.6 0.7 slice.52
  213.3 1.6 slice_reduce_fusion
  214.9 0.6 reshape.73
  215.5 0.0 copy-start.7
  215.5 1.2 fusion
  216.7 0.0 copy-start.6
  216.7 1.1 maximum_convert_fusion.2
  217.8 0.0 copy-done.7
  217.8 0.7 copy-done.6
  218.5 0.0 copy-start.4
  218.5 0.0 copy-start.5
  218.5 1.9 slice_convert_fusion.1
  220.4 0.0 copy-done.4
  220.4 1.0 copy-done.5
  221.4 0.0 copy-start.2
  221.4 0.0 copy-start.3
  221.4 2.8 %maximum_convert_fusion = f32[768,1536]{1,0:T(8,128)} fusion(bf16[768,768]{1,0:T(8,128)(2,1)S(1)} %copy-done.5, bf16[768,768]{1,0:T(8,128)(2,1)S(1)} %copy-done.4), kind=kLoop, calls=%fused_computation | loop fusion | flops 4718592 | bytes 7077888 | tf_op jit(solution)/shard_map/convert_element_type | solution.py:699
  224.2 0.0 copy-done.2
  224.2 0.0 copy-done.3
  224.2 0.0 copy-start.1
  224.2 2.5 %maximum_convert_fusion.1 = f32[1536,768]{1,0:T(8,128)} fusion(bf16[768,768]{1,0:T(8,128)(2,1)S(1)} %copy-done.3, bf16[768,768]{1,0:T(8,128)(2,1)S(1)} %copy-done.2), kind=kLoop, calls=%fused_computation.1 | loop fusion | flops 4718592 | bytes 7077888 | tf_op jit(solution)/shard_map/convert_element_type | solution.py:699
  226.8 0.0 copy-done.1
  226.8 0.0 copy-start
  226.8 1.1 copy.37
  227.9 0.8 copy-done
  228.8 1.1 copy.38
Async XLA Ops:
  215.5 2.3 %copy-start.7 = (bf16[768,768]{1,0:T(8,128)(2,1)S(1)}, bf16[768,768]{1,0:T(8,128)(2,1)}, u32[]{:S(2)}) copy-start(bf16[768,768]{1,0:T(8,128)(2,1)} %get-tuple-element.28) | copy-start | bytes 3538948
  216.7 1.8 copy-start.6
  218.5 1.9 copy-start.4
  218.5 2.9 %copy-start.5 = (bf16[768,768]{1,0:T(8,128)(2,1)S(1)}, bf16[768,768]{1,0:T(8,128)(2,1)}, u32[]{:S(2)}) copy-start(bf16[768,768]{1,0:T(8,128)(2,1)} %get-tuple-element.32) | copy-start | bytes 3538948
  221.4 2.8 %copy-start.2 = (bf16[768,768]{1,0:T(8,128)(2,1)S(1)}, bf16[768,768]{1,0:T(8,128)(2,1)}, u32[]{:S(2)}) copy-start(bf16[768,768]{1,0:T(8,128)(2,1)} %get-tuple-element.33) | copy-start | bytes 3538948
  221.4 2.8 %copy-start.3 = (bf16[768,768]{1,0:T(8,128)(2,1)S(1)}, bf16[768,768]{1,0:T(8,128)(2,1)}, u32[]{:S(2)}) copy-start(bf16[768,768]{1,0:T(8,128)(2,1)} %get-tuple-element.34) | copy-start | bytes 3538948
  224.2 2.6 %copy-start.1 = (bf16[1024,768]{1,0:T(8,128)(2,1)S(1)}, bf16[1024,768]{1,0:T(8,128)(2,1)}, u32[]{:S(2)}) copy-start(bf16[1024,768]{1,0:T(8,128)(2,1)} %get-tuple-element.65) | copy-start | bytes 4718596
  226.8 2.0 copy-start
